TPU v7x, 128 devices: a whole 4x4x4 slice. The times are simulated.
128 devices in a mesh: expert: 32 (over y, x, core), fsdp: 4 (over z).
Axes of the slice: x: 4, y: 4, z: 4, core: 2. Of those that a mesh axis runs over, the one named last changes fastest.
Arguments:
- tokens: bfloat16 [32768, 1024], P(('expert', 'fsdp')), may hold values from -6 to 6
- segments: int32 [32768], P(('expert', 'fsdp')), may hold values from 0 to 95, as said below
- positions: int32 [32768], P(('expert', 'fsdp')), may hold values from 0 to 1021, as said below
- routes: int32 [32768, 8], P(('expert', 'fsdp')), may hold values from 0 to 31, all different within a row; in each aligned block of 256 rows (0 to 255, 256 to 511, ...) at most 96 rows name the same one
- w_query: bfloat16 [1024, 1024], P(('expert', 'fsdp')), may hold values from -0.1875 to 0.1875
- w_key: bfloat16 [1024, 512], P(('expert', 'fsdp')), may hold values from -0.1875 to 0.1875
- w_value: bfloat16 [1024, 512], P(('expert', 'fsdp')), may hold values from -0.1875 to 0.1875
- w_output: bfloat16 [1024, 1024], P(('expert', 'fsdp')), may hold values from -1.5 to 1.5
- w_router: bfloat16 [1024, 32], P(('expert', 'fsdp')), may hold values from -0.09375 to 0.09375
- w_gate: bfloat16 [32, 1024, 512], P('expert', 'fsdp'), may hold values from -0.1875 to 0.1875
- w_up: bfloat16 [32, 1024, 512], P('expert', 'fsdp'), may hold values from -0.1875 to 0.1875
- w_down: bfloat16 [32, 512, 1024], P('expert', 'fsdp'), may hold values from -4 to 4
- g_attn: float32 [1024], replicated, may hold values from 0.5 to 1.5
- g_ffn: float32 [1024], replicated, may hold values from 0.5 to 1.5
- g_query: float32 [64], replicated, may hold values from 0.1 to 1.9
- g_key: float32 [64], replicated, may hold values from 0.1 to 1.9
- cotangent: bfloat16 [32768, 1024], P(('expert', 'fsdp')), may hold values from -6 to 6
Outputs:
- output: bfloat16 [32768, 1024], P(('expert', 'fsdp'))
- grad_tokens: bfloat16 [32768, 1024], P(('expert', 'fsdp'))
- grad_query: float32 [1024, 1024], P(('expert', 'fsdp'))
- grad_key: float32 [1024, 512], P(('expert', 'fsdp'))
- grad_value: float32 [1024, 512], P(('expert', 'fsdp'))
- grad_output: float32 [1024, 1024], P(('expert', 'fsdp'))
- grad_router: float32 [1024, 32], P(('expert', 'fsdp'))
- grad_gate: float32 [32, 1024, 512], P('expert', 'fsdp')
- grad_up: float32 [32, 1024, 512], P('expert', 'fsdp')
- grad_down: float32 [32, 512, 1024], P('expert', 'fsdp')
- grad_g_attn: float32 [1024], replicated
- grad_g_ffn: float32 [1024], replicated
- grad_g_query: float32 [64], replicated
- grad_g_key: float32 [64], replicated
Inputs may be any that keep to these rules, and one draw needn't show every extreme that they name: `segments`: numbers never fall along the tokens; each sequence of 1024 tokens holds three documents of its own. `positions`: each token's offset from the first token of its document. `routes`: each row names 8 different experts; the 256 rows of one device name no expert more than 96 times, and in some devices' rows some expert exactly 96 times.
All inputs are finite; a program needn't handle non-finite values.
Results may differ from a plain program's by a relative error of at most 0.02.
Values may be sent and summed in bfloat16 or wider, within the bound.
No kernel may reach another device: no remote copies, remote signals or barrier semaphores. Data moves between devices by JAX's collectives and lax.ppermute only.
A program may use at most 192 MiB of HBM per device.

v0:
```python
from functools import partial
import math

import jax
import jax.numpy as jnp
from jax import lax
from jax.sharding import PartitionSpec as P

HEAD = 64
EXPERTS = 32
TOP = 8
MOST = 96


EPS = 1e-06
NEG = -1e30


def rms_scale(values, gain):
    return values * lax.rsqrt(jnp.mean(values * values, axis=-1, keepdims=True) + EPS) * gain


def rotate(values, cosine, sine):
    half = values.shape[-1] // 2
    first = values[..., :half]
    second = values[..., half:]
    return jnp.concatenate(
        [first * cosine - second * sine, second * cosine + first * sine], axis=-1
    )


def rotation(position):
    steps = jnp.arange(HEAD // 2, dtype=jnp.float32)
    freq = jnp.exp(steps * (-2.0 * math.log(10000.0) / HEAD))
    angle = position.astype(jnp.float32)[:, None] * freq[None, :]
    return (jnp.cos(angle)[:, None, :], jnp.sin(angle)[:, None, :])


def prepare_heads(q_raw, k_raw, g_query, g_key, cosine, sine):
    length = q_raw.shape[0]
    queries = rotate(rms_scale(q_raw.reshape(length, -1, HEAD), g_query), cosine, sine)
    keys = rotate(rms_scale(k_raw.reshape(length, -1, HEAD), g_key), cosine, sine)
    return (queries, keys)


def route_gates(logits, chosen):
    return jnp.sum(chosen * jax.nn.softmax(logits, axis=-1)[:, None, :], axis=-1)


def swiglu(gate_pre, up_pre):
    return jax.nn.silu(gate_pre) * up_pre


def rounded(values):
    return lax.optimization_barrier(values.astype(jnp.bfloat16)).astype(jnp.float32)


def per_device(
    tokens,
    segments,
    positions,
    routes,
    w_query,
    w_key,
    w_value,
    w_output,
    w_router,
    w_gate,
    w_up,
    w_down,
    g_attn,
    g_ffn,
    g_query,
    g_key,
    cotangent,
):
    rows = tokens.shape[0]
    groups = lax.axis_size("expert")
    local_experts = w_gate.shape[0]
    scale = HEAD ** (-0.5)
    full_q, full_k, full_v, full_o, full_router = (
        lax.all_gather(w_query, ("expert", "fsdp"), axis=0, tiled=True),
        lax.all_gather(w_key, ("expert", "fsdp"), axis=0, tiled=True),
        lax.all_gather(w_value, ("expert", "fsdp"), axis=0, tiled=True),
        lax.all_gather(w_output, ("expert", "fsdp"), axis=0, tiled=True),
        lax.all_gather(w_router, ("expert", "fsdp"), axis=0, tiled=True),
    )
    inputs = tokens.astype(jnp.float32)
    normed_first, first_back = jax.vjp(rms_scale, inputs, g_attn)
    first_low = normed_first.astype(jnp.bfloat16)
    q_raw = jnp.dot(first_low, full_q, preferred_element_type=jnp.float32)
    k_raw = jnp.dot(first_low, full_k, preferred_element_type=jnp.float32)
    value_low = jnp.dot(first_low, full_v, preferred_element_type=jnp.float32).astype(jnp.bfloat16)
    cosine, sine = rotation(positions)
    (query_f, key_f), prep_back = jax.vjp(
        partial(prepare_heads, cosine=cosine, sine=sine), q_raw, k_raw, g_query, g_key
    )
    query_low = query_f.astype(jnp.bfloat16)
    key_low = key_f.astype(jnp.bfloat16)
    kv_heads = key_low.shape[1]
    key_flat, value_flat = (
        lax.all_gather(key_low.reshape(rows, -1), "fsdp", axis=0, tiled=True),
        lax.all_gather(value_low, "fsdp", axis=0, tiled=True),
    )
    key_all = key_flat.reshape(key_flat.shape[0], kv_heads, HEAD)
    value_all = value_flat.reshape(value_flat.shape[0], kv_heads, HEAD)
    grouped = query_low.reshape(rows, kv_heads, -1, HEAD)
    query_index = lax.axis_index("fsdp") * rows + jnp.arange(rows, dtype=jnp.int32)
    key_index = jnp.arange(key_all.shape[0], dtype=jnp.int32)
    distance = query_index[:, None] - key_index[None, :]
    allowed = (distance >= 0) & (distance <= positions[:, None])

    def masked_scores():
        raw = (
            jnp.einsum("qkgd,skd->kgqs", grouped, key_all, preferred_element_type=jnp.float32)
            * scale
        )
        return jnp.where(allowed, raw, NEG)

    scores = masked_scores()
    largest = jnp.max(scores, axis=-1, keepdims=True)
    log_total = largest + jnp.log(jnp.sum(jnp.exp(scores - largest), axis=-1, keepdims=True))
    probs_low = jnp.exp(scores - log_total).astype(jnp.bfloat16)
    mixed_low = (
        jnp.einsum("kgqs,skd->qkgd", probs_low, value_all, preferred_element_type=jnp.float32)
        .reshape(rows, -1)
        .astype(jnp.bfloat16)
    )
    middle = inputs + jnp.dot(mixed_low, full_o, preferred_element_type=jnp.float32)
    normed_second, second_back = jax.vjp(rms_scale, middle, g_ffn)
    second_low = normed_second.astype(jnp.bfloat16)
    logits = jnp.dot(second_low, full_router, preferred_element_type=jnp.float32)
    chosen = (routes[:, :, None] == jnp.arange(EXPERTS, dtype=jnp.int32)[None, None, :]).astype(
        jnp.float32
    )
    gates, gates_back = jax.vjp(partial(route_gates, chosen=chosen), logits)
    pairs = rows * TOP
    expert_of = routes.reshape(pairs)
    hits = (expert_of[:, None] == jnp.arange(EXPERTS, dtype=jnp.int32)[None, :]).astype(jnp.int32)
    slot = jnp.sum((jnp.cumsum(hits, axis=0) - hits) * hits, axis=1)
    target = expert_of * MOST + slot
    pair_ids = jnp.arange(pairs, dtype=jnp.int32)
    source_row = jnp.full((EXPERTS * MOST,), rows, jnp.int32).at[target].set(pair_ids // TOP)
    pair_row = jnp.full((EXPERTS * MOST,), pairs, jnp.int32).at[target].set(pair_ids)
    width = second_low.shape[1]
    padded_rows = jnp.concatenate([second_low, jnp.zeros((1, width), jnp.bfloat16)], axis=0)
    outgoing = padded_rows[source_row].reshape(groups, local_experts * MOST, width)
    incoming = lax.all_to_all(outgoing, "expert", split_axis=0, concat_axis=0, tiled=True).reshape(
        groups, local_experts, MOST, width
    )
    gate_full, up_full, down_full = (
        lax.all_gather(w_gate, "fsdp", axis=1, tiled=True),
        lax.all_gather(w_up, "fsdp", axis=1, tiled=True),
        lax.all_gather(w_down, "fsdp", axis=1, tiled=True),
    )
    gate_pre = jnp.einsum("sepd,edf->sepf", incoming, gate_full, preferred_element_type=jnp.float32)
    up_pre = jnp.einsum("sepd,edf->sepf", incoming, up_full, preferred_element_type=jnp.float32)
    hidden, swiglu_back = jax.vjp(swiglu, gate_pre, up_pre)
    hidden_low = hidden.astype(jnp.bfloat16)
    expert_out = jnp.einsum(
        "sepf,efd->sepd", hidden_low, down_full, preferred_element_type=jnp.float32
    ).astype(jnp.bfloat16)
    returned = lax.all_to_all(
        expert_out.reshape(groups, local_experts * MOST, width),
        "expert",
        split_axis=0,
        concat_axis=0,
        tiled=True,
    )
    per_pair = returned.reshape(EXPERTS * MOST, width)[target].reshape(rows, TOP, width)
    mixture = jnp.einsum("rt,rtd->rd", gates, per_pair, preferred_element_type=jnp.float32)
    output = (middle + mixture).astype(jnp.bfloat16)
    grad_out = cotangent.astype(jnp.float32)
    grad_gates = jnp.einsum("rtd,rd->rt", per_pair, grad_out, preferred_element_type=jnp.float32)
    pair_grads = (
        (gates[:, :, None] * grad_out[:, None, :]).astype(jnp.bfloat16).reshape(pairs, width)
    )
    padded_grads = jnp.concatenate([pair_grads, jnp.zeros((1, width), jnp.bfloat16)], axis=0)
    sent_grads = padded_grads[pair_row].reshape(groups, local_experts * MOST, width)
    grads_in = lax.all_to_all(
        sent_grads, "expert", split_axis=0, concat_axis=0, tiled=True
    ).reshape(groups, local_experts, MOST, width)
    gate_back_w, up_back_w, down_back_w = (
        lax.all_gather(w_gate, "fsdp", axis=1, tiled=True),
        lax.all_gather(w_up, "fsdp", axis=1, tiled=True),
        lax.all_gather(w_down, "fsdp", axis=1, tiled=True),
    )
    grad_hidden = rounded(
        jnp.einsum("sepd,efd->sepf", grads_in, down_back_w, preferred_element_type=jnp.float32)
    )
    grad_gate_pre, grad_up_pre = swiglu_back(grad_hidden)
    grad_gate_low = grad_gate_pre.astype(jnp.bfloat16)
    grad_up_low = grad_up_pre.astype(jnp.bfloat16)
    grad_rows = jnp.einsum(
        "sepf,edf->sepd", grad_gate_low, gate_back_w, preferred_element_type=jnp.float32
    )
    grad_rows = (
        grad_rows
        + jnp.einsum("sepf,edf->sepd", grad_up_low, up_back_w, preferred_element_type=jnp.float32)
    ).astype(jnp.bfloat16)
    grad_gate_w = jnp.einsum(
        "sepd,sepf->edf", incoming, grad_gate_low, preferred_element_type=jnp.float32
    )
    grad_up_w = jnp.einsum(
        "sepd,sepf->edf", incoming, grad_up_low, preferred_element_type=jnp.float32
    )
    grad_down_w = jnp.einsum(
        "sepf,sepd->efd", hidden_low, grads_in, preferred_element_type=jnp.float32
    )
    expert_sums = (
        lax.psum_scatter(grad_gate_w, "fsdp", scatter_dimension=1, tiled=True),
        lax.psum_scatter(grad_up_w, "fsdp", scatter_dimension=1, tiled=True),
        lax.psum_scatter(grad_down_w, "fsdp", scatter_dimension=1, tiled=True),
    )
    back_rows = lax.all_to_all(
        grad_rows.reshape(groups, local_experts * MOST, width),
        "expert",
        split_axis=0,
        concat_axis=0,
        tiled=True,
    )
    pair_back = back_rows.reshape(EXPERTS * MOST, width)[target].reshape(rows, TOP, width)
    grad_second = jnp.sum(pair_back, axis=1, dtype=jnp.float32)
    back_q, back_k, back_v, back_o, back_router = (
        lax.all_gather(w_query, ("expert", "fsdp"), axis=0, tiled=True),
        lax.all_gather(w_key, ("expert", "fsdp"), axis=0, tiled=True),
        lax.all_gather(w_value, ("expert", "fsdp"), axis=0, tiled=True),
        lax.all_gather(w_output, ("expert", "fsdp"), axis=0, tiled=True),
        lax.all_gather(w_router, ("expert", "fsdp"), axis=0, tiled=True),
    )
    grad_logits_low = gates_back(grad_gates)[0].astype(jnp.bfloat16)
    grad_second = grad_second + jnp.dot(
        grad_logits_low, back_router.T, preferred_element_type=jnp.float32
    )
    grad_router_w = jnp.dot(second_low.T, grad_logits_low, preferred_element_type=jnp.float32)
    grad_middle_norm, grad_g_ffn = second_back(grad_second)
    grad_middle = grad_out + grad_middle_norm
    grad_attention_low = grad_middle.astype(jnp.bfloat16)
    grad_o_w = jnp.dot(mixed_low.T, grad_attention_low, preferred_element_type=jnp.float32)
    grad_mixed = (
        jnp.dot(grad_attention_low, back_o.T, preferred_element_type=jnp.float32)
        .astype(jnp.bfloat16)
        .reshape(rows, kv_heads, -1, HEAD)
    )
    probs = jnp.exp(masked_scores() - log_total)
    grad_probs = jnp.einsum(
        "qkgd,skd->kgqs", grad_mixed, value_all, preferred_element_type=jnp.float32
    )
    delta = jnp.sum(probs * grad_probs, axis=-1, keepdims=True)
    grad_scores_low = (probs * (grad_probs - delta)).astype(jnp.bfloat16)
    grad_query_heads = (
        jnp.einsum("kgqs,skd->qkgd", grad_scores_low, key_all, preferred_element_type=jnp.float32)
        * scale
    )
    grad_key_all = (
        jnp.einsum("kgqs,qkgd->skd", grad_scores_low, grouped, preferred_element_type=jnp.float32)
        * scale
    )
    grad_value_all = jnp.einsum(
        "kgqs,qkgd->skd", probs.astype(jnp.bfloat16), grad_mixed, preferred_element_type=jnp.float32
    )
    grad_key_mine, grad_value_mine = (
        lax.psum_scatter(
            grad_key_all.reshape(grad_key_all.shape[0], -1), "fsdp", scatter_dimension=0, tiled=True
        ),
        lax.psum_scatter(
            grad_value_all.reshape(grad_value_all.shape[0], -1),
            "fsdp",
            scatter_dimension=0,
            tiled=True,
        ),
    )
    grad_value_low = grad_value_mine.astype(jnp.bfloat16)
    grad_q_raw, grad_k_raw, grad_g_query, grad_g_key = prep_back(
        (
            rounded(grad_query_heads.reshape(rows, -1, HEAD)),
            rounded(grad_key_mine.reshape(rows, kv_heads, HEAD)),
        )
    )
    grad_q_low = grad_q_raw.astype(jnp.bfloat16)
    grad_k_low = grad_k_raw.astype(jnp.bfloat16)
    grad_first = jnp.dot(grad_q_low, back_q.T, preferred_element_type=jnp.float32)
    grad_first = grad_first + jnp.dot(grad_k_low, back_k.T, preferred_element_type=jnp.float32)
    grad_first = grad_first + jnp.dot(grad_value_low, back_v.T, preferred_element_type=jnp.float32)
    grad_inputs_norm, grad_g_attn = first_back(grad_first)
    grad_tokens = (grad_middle + grad_inputs_norm).astype(jnp.bfloat16)
    grad_q_w = jnp.dot(first_low.T, grad_q_low, preferred_element_type=jnp.float32)
    grad_k_w = jnp.dot(first_low.T, grad_k_low, preferred_element_type=jnp.float32)
    grad_v_w = jnp.dot(first_low.T, grad_value_low, preferred_element_type=jnp.float32)
    dense_sums = (
        lax.psum_scatter(grad_q_w, ("expert", "fsdp"), scatter_dimension=0, tiled=True),
        lax.psum_scatter(grad_k_w, ("expert", "fsdp"), scatter_dimension=0, tiled=True),
        lax.psum_scatter(grad_v_w, ("expert", "fsdp"), scatter_dimension=0, tiled=True),
        lax.psum_scatter(grad_o_w, ("expert", "fsdp"), scatter_dimension=0, tiled=True),
        lax.psum_scatter(grad_router_w, ("expert", "fsdp"), scatter_dimension=0, tiled=True),
    )
    gain_sums = lax.psum((grad_g_attn, grad_g_ffn, grad_g_query, grad_g_key), ("expert", "fsdp"))
    return (
        output,
        grad_tokens,
        dense_sums[0],
        dense_sums[1],
        dense_sums[2],
        dense_sums[3],
        dense_sums[4],
        expert_sums[0],
        expert_sums[1],
        expert_sums[2],
        gain_sums[0],
        gain_sums[1],
        gain_sums[2],
        gain_sums[3],
    )


def solution(mesh):
    in_specs = (
        P(("expert", "fsdp"), None),
        P(("expert", "fsdp")),
        P(("expert", "fsdp")),
        P(("expert", "fsdp"), None),
        P(("expert", "fsdp"), None),
        P(("expert", "fsdp"), None),
        P(("expert", "fsdp"), None),
        P(("expert", "fsdp"), None),
        P(("expert", "fsdp"), None),
        P("expert", "fsdp", None),
        P("expert", "fsdp", None),
        P("expert", "fsdp", None),
        P(),
        P(),
        P(),
        P(),
        P(("expert", "fsdp"), None),
    )
    out_specs = (
        P(("expert", "fsdp"), None),
        P(("expert", "fsdp"), None),
        P(("expert", "fsdp"), None),
        P(("expert", "fsdp"), None),
        P(("expert", "fsdp"), None),
        P(("expert", "fsdp"), None),
        P(("expert", "fsdp"), None),
        P("expert", "fsdp", None),
        P("expert", "fsdp", None),
        P("expert", "fsdp", None),
        P(),
        P(),
        P(),
        P(),
    )
    return jax.shard_map(
        per_device, mesh=mesh, in_specs=in_specs, out_specs=out_specs, check_vma=False
    )
```

profile of v0, /device:TPU:0, one launch (start us, length us, event | category | flops | bytes accessed | tf_op | source)
XLA Modules:
  0.0 3720.8 jit_solution(5693164015781049132)
XLA Ops:
  10.0 66.9 %all-gather.10.cloned.1.call-done = bf16[1024,512]{1,0:T(8,128)(2,1)} async-done(((bf16[8,512]{1,0:T(8,128)(2,1)}), bf16[1024,512]{1,0:T(8,128)(2,1)}) %all-gather.10.cloned.1.call-update) | async-done | bytes 1048592 | tf_op jit(solution)/shard_map/all_gather | solution.py:84
  76.9 2.6 convolution_convert_fusion.2
  81.1 59.7 %all-gather.14.cloned.1.call-done = bf16[1024,512]{1,0:T(8,128)(2,1)} async-done(((bf16[8,512]{1,0:T(8,128)(2,1)}), bf16[1024,512]{1,0:T(8,128)(2,1)}) %all-gather.14.cloned.1.call-update) | async-done | bytes 1048592 | tf_op jit(solution)/shard_map/all_gather | solution.py:83
  140.7 2.0 multiply_reduce_fusion.8
  146.4 9.1 reduce-window.6
  156.4 8.3 scatter_custom_fusion
  166.5 66.5 %all-gather.18.cloned.1.call-done = bf16[1024,1024]{1,0:T(8,128)(2,1)} async-done(((bf16[8,1024]{1,0:T(8,128)(2,1)}), bf16[1024,1024]{1,0:T(8,128)(2,1)}) %all-gather.18.cloned.1.call-update) | async-done | bytes 2097168 | tf_op jit(solution)/shard_map/all_gather | solution.py:82
  233.0 2.6 multiply_reduce_fusion.5
  237.0 21.6 all-gather.16.cloned.1.call-done
  258.6 8.6 fusion.97
  267.2 8.1 exponential_reduce_fusion
  275.3 8.4 fusion.31
  283.7 43.7 %all-gather.20.cloned.1.call-done = bf16[1024,1024]{1,0:T(8,128)(2,1)} async-done(((bf16[8,1024]{1,0:T(8,128)(2,1)}), bf16[1024,1024]{1,0:T(8,128)(2,1)}) %all-gather.20.cloned.1.call-update) | async-done | bytes 2097168 | tf_op jit(solution)/shard_map/all_gather | solution.py:85
  327.5 2.4 multiply_reduce_fusion.4
  330.1 13.9 gather_fusion
  344.1 5.0 all-to-all-start
  351.3 24.4 all-gather.22.cloned.1.call-done
  375.7 51.3 %all-to-all-done = bf16[32,96,1024]{2,1,0:T(8,128)(2,1)} async-done(((bf16[32,96,1024]{2,1,0:T(8,128)(2,1)}), bf16[32,96,1024]{2,1,0:T(8,128)(2,1)}, u32[]{:S(2)}, u32[]{:S(2)}) %all-to-all-start) | async-done | bytes 6291488 | tf_op jit(solution)/shard_map/all_to_all | solution.py:148
  427.0 9.1 fusion.51
  436.1 6.0 fusion.48
  442.1 2.6 copy-done.4
  444.7 3.2 fusion.17
  447.9 8.3 convolution_convert_fusion
  456.2 5.0 all-to-all-start.1
  461.3 8.1 scatter_custom_fusion.1
  469.4 113.4 %all_gather.44 = bf16[1024,32]{1,0:T(8,128)(2,1)S(1)} all-gather(bf16[8,32]{1,0:T(8,128)(2,1)S(1)} %copy-done.54), channel_id=1, replica_groups=mesh['expert'=32,'fsdp'=4] {'expert','fsdp'}, dimensions={0}, use_global_device_ids=true | all-gather | bytes 66048 | tf_op jit(solution)/shard_map/all_gather | solution.py:86
  583.2 14.6 gather_fusion.1
  597.8 4.5 fusion.13
  603.4 2.4 concatenate.24
  605.8 18.7 gather_fusion.2
  624.5 79.7 %all_to_all.20 = bf16[32,96,1024]{2,1,0:T(8,128)(2,1)S(1)} all-to-all(bf16[32,96,1024]{2,1,0:T(8,128)(2,1)} %bitcast.233), channel_id=1, replica_groups=mesh['expert'=32,'fsdp'=4] {'expert'}, dimensions={0} | all-to-all | bytes 12582912 | tf_op jit(solution)/shard_map/all_to_all | solution.py:180
  704.2 4.0 convert_bitcast_fusion
  708.7 2.7 fusion.8
  711.4 1.7 copy-done.18
  713.0 6.6 fusion.21
  719.6 12.7 add_convert_fusion
  732.3 4.9 all-to-all-start.3
  737.7 4.4 fusion.15
  742.1 73.0 %all-to-all-done.3 = bf16[32,96,1024]{2,1,0:T(8,128)(2,1)} async-done(((bf16[32,96,1024]{2,1,0:T(8,128)(2,1)}), bf16[32,96,1024]{2,1,0:T(8,128)(2,1)}, u32[]{:S(2)}, u32[]{:S(2)}) %all-to-all-start.3) | async-done | bytes 6291488 | tf_op jit(solution)/shard_map/all_to_all | solution.py:215
  815.1 14.6 gather_fusion.3
  829.7 5.6 convert_reduce_fusion
  838.1 9.9 fusion.23
  848.6 10.7 fusion
  859.2 7.7 fusion.2
  867.0 4.0 bitcast_multiply_fusion.5
  872.3 8.6 convolution_bitcast_fusion
  881.0 10.9 convolution_bitcast_fusion.1
  892.1 8.6 fusion.27
  900.9 3.1 fusion.65
  904.0 1.5 reduce-scatter.10.cloned.1.call-done
  907.7 1.9 fusion.88
  909.7 2.7 fusion.61
  912.5 5.3 fusion.30
  918.9 2.8 fusion.90
  921.7 132.7 %all-reduce.10.cloned.1.call-done = f32[1024,32]{1,0:T(8,128)} async-done(((f32[1024,32]{1,0:T(8,128)}), f32[1024,32]{1,0:T(8,128)}) %all-reduce.10.cloned.1.call-update) | async-done | bytes 131088
  1055.7 2.3 fusion.99
  1058.0 1.7 convolution_add_fusion.1
  1059.8 2.1 fusion.37
  1061.9 67.2 %all-reduce.7 = (f32[1024]{0:T(1024)}, f32[1024]{0:T(1024)}, f32[64]{0:T(128)}, f32[64]{0:T(128)}) all-reduce(f32[1024]{0:T(1024)S(1)} %get-tuple-element.16, f32[1024]{0:T(1024)S(1)} %get-tuple-element.14, f32[64]{0:T(128)S(1)} %get-tuple-element.18, f32[64]{0:T(128)S(1)} %copy-done.55), channel_id=1, replica_groups=mesh['expert'=32,'fsdp'=4] {'expert','fsdp'}, use_global_device_ids=true, to_apply=%region_33.34 | all-reduce | flops 2176 | bytes 17408 | tf_op jit(solution)/shard_map/psum | solution.py:297
  1130.2 22.1 reduce-scatter.22.cloned.1.call-done
  1152.3 643.7 %reduce-scatter.18.cloned.1.call-done = f32[8,512]{1,0:T(8,128)} async-done(((f32[1024,512]{1,0:T(8,128)}), f32[8,512]{1,0:T(8,128)}) %reduce-scatter.18.cloned.1.call-update) | async-done | bytes 16400 | tf_op jit(solution)/shard_map/reduce_scatter | solution.py:293
  1796.0 637.9 %reduce-scatter.16.cloned.1.call-done = f32[8,512]{1,0:T(8,128)} async-done(((f32[1024,512]{1,0:T(8,128)}), f32[8,512]{1,0:T(8,128)}) %reduce-scatter.16.cloned.1.call-update) | async-done | bytes 16400 | tf_op jit(solution)/shard_map/reduce_scatter | solution.py:292
  2433.9 640.0 %reduce-scatter.20.cloned.1.call-done = f32[8,1024]{1,0:T(8,128)} async-done(((f32[1024,1024]{1,0:T(8,128)}), f32[8,1024]{1,0:T(8,128)}) %reduce-scatter.20.cloned.1.call-update) | async-done | bytes 32784 | tf_op jit(solution)/shard_map/reduce_scatter | solution.py:294
  3073.9 640.2 %reduce-scatter.14.cloned.1.call-done = f32[8,1024]{1,0:T(8,128)} async-done(((f32[1024,1024]{1,0:T(8,128)}), f32[8,1024]{1,0:T(8,128)}) %reduce-scatter.14.cloned.1.call-update) | async-done | bytes 32784 | tf_op jit(solution)/shard_map/reduce_scatter | solution.py:291
  (240 shorter events, 27.2 us)
Async XLA Ops:
  7.2 157.5 %copy-start.53 = (s32[256]{0:T(256)S(1)}, s32[256]{0:T(256)}, u32[]{:S(2)}) copy-start(s32[256]{0:T(256)} %param.18) | copy-start | bytes 3076
  7.2 138.6 %copy-start.40 = (s32[256,8]{0,1:T(8,128)S(1)}, s32[256,8]{0,1:T(8,128)}, u32[]{:S(2)}) copy-start(s32[256,8]{0,1:T(8,128)} %param.19) | copy-start | bytes 24580
  7.2 69.7 %all-gather.10.cloned.1.call-start = ((), (), s32[]{:S(2)}) async-start(), calls=%async_computation.13 | async-start | bytes 1056768 | tf_op jit(solution)/shard_map/all_gather | solution.py:84
  7.9 132.8 %all-gather.14.cloned.1.call-start = ((), (), s32[]{:S(2)}) async-start(), calls=%async_computation.15 | async-start | bytes 1056768 | tf_op jit(solution)/shard_map/all_gather | solution.py:83
  8.7 156.3 %all-gather.12.cloned.1.call-start = ((), (), s32[]{:S(2)}) async-start(), calls=%async_computation.14 | async-start | bytes 1310720 | tf_op jit(solution)/shard_map/all_gather | solution.py:103
  10.0 156.5 %copy-start.48 = (f32[256]{0:T(256)}, f32[256]{0:T(256)S(1)}, u32[]{:S(2)}) copy-start(f32[256]{0:T(256)S(1)} %fusion.42) | copy-start | bytes 3076
  10.0 223.0 %copy-start.44 = (f32[256]{0:T(256)}, f32[256]{0:T(256)S(1)}, u32[]{:S(2)}) copy-start(f32[256]{0:T(256)S(1)} %fusion.81) | copy-start | bytes 3076
  10.0 223.0 %copy-start.1 = (bf16[256,1024]{1,0:T(8,128)(2,1)S(1)}, bf16[256,1024]{1,0:T(8,128)(2,1)}, u32[]{:S(2)}) copy-start(bf16[256,1024]{1,0:T(8,128)(2,1)} %param.17) | copy-start | bytes 1572868
  10.0 223.0 %copy-start.38 = (f32[1024]{0:T(1024)S(1)}, f32[1024]{0:T(1024)}, u32[]{:S(2)}) copy-start(f32[1024]{0:T(1024)} %param.28) | copy-start | bytes 12292
  79.5 153.4 %all-gather.18.cloned.1.call-start = ((), (), s32[]{:S(2)}) async-start(), calls=%async_computation.17 | async-start | bytes 2113536 | tf_op jit(solution)/shard_map/all_gather | solution.py:82
  80.1 178.5 %all-gather.16.cloned.1.call-start = ((), (), s32[]{:S(2)}) async-start(), calls=%async_computation.16 | async-start | bytes 1310720 | tf_op jit(solution)/shard_map/all_gather | solution.py:102
  81.0 155.7 %copy-start.26 = (f32[256,32]{0,1:T(8,128)}, f32[256,32]{0,1:T(8,128)S(1)}, u32[]{:S(2)}) copy-start(f32[256,32]{0,1:T(8,128)S(1)} %get-tuple-element.38) | copy-start | bytes 98308
  81.0 155.7 %copy-start.28 = (f32[256,32]{0,1:T(8,128)}, f32[256,32]{0,1:T(8,128)S(1)}, u32[]{:S(2)}) copy-start(f32[256,32]{0,1:T(8,128)S(1)} %get-tuple-element.39) | copy-start | bytes 98308
  142.8 13.6 copy-start.46
  142.8 93.8 %copy-start.51 = (f32[64]{0:T(128)S(1)}, f32[64]{0:T(128)}, u32[]{:S(2)}) copy-start(f32[64]{0:T(128)} %param.30) | copy-start | bytes 772
  145.1 182.3 %all-gather.20.cloned.1.call-start = ((), (), s32[]{:S(2)}) async-start(), calls=%async_computation.18 | async-start | bytes 2113536 | tf_op jit(solution)/shard_map/all_gather | solution.py:85
  166.5 108.8 %copy-start.7 = (bf16[1024,512]{0,1:T(8,128)(2,1)}, bf16[1024,512]{0,1:T(8,128)(2,1)S(1)}, u32[]{:S(2)}) copy-start(bf16[1024,512]{0,1:T(8,128)(2,1)S(1)} %copy.75) | copy-start | bytes 3145732
  236.9 30.2 copy-start.20
  237.0 30.2 copy-start.22
  275.2 8.5 copy-start.30
  275.3 54.7 %copy-start.43 = (f32[1024]{0:T(1024)S(1)}, f32[1024]{0:T(1024)}, u32[]{:S(2)}) copy-start(f32[1024]{0:T(1024)} %param.29) | copy-start | bytes 12292
  283.7 46.2 %copy-start.15 = (bf16[8,64,2,256]{3,1,2,0:T(8,128)(2,1)}, bf16[8,64,2,256]{3,1,2,0:T(8,128)(2,1)S(1)}, u32[]{:S(2)}) copy-start(bf16[8,64,2,256]{3,1,2,0:T(8,128)(2,1)S(1)} %fusion.31) | copy-start | bytes 1572868
  330.1 252.7 %copy-start.9 = (bf16[256,1024]{1,0:T(8,128)(2,1)}, bf16[256,1024]{1,0:T(8,128)(2,1)S(1)}, u32[]{:S(2)}) copy-start(bf16[256,1024]{1,0:T(8,128)(2,1)S(1)} %multiply_convert_fusion) | copy-start | bytes 1572868
  344.1 82.9 %all-to-all-start = ((bf16[32,96,1024]{2,1,0:T(8,128)(2,1)}), bf16[32,96,1024]{2,1,0:T(8,128)(2,1)}, u32[]{:S(2)}, u32[]{:S(2)}) async-start(bf16[32,96,1024]{2,1,0:T(8,128)(2,1)} %bitcast.232), calls=%async_computation | async-start | bytes 12582912 | tf_op jit(solution)/shard_map/all_to_all | solution.py:148
  349.1 26.6 all-gather.22.cloned.1.call-start
  349.9 86.2 %all-gather.24.cloned.1.call-start = ((), (), s32[]{:S(2)}) async-start(), calls=%async_computation.20 | async-start | bytes 1310720 | tf_op jit(solution)/shard_map/all_gather | solution.py:153
  350.6 97.3 %all-gather.26.cloned.1.call-start = ((), (), s32[]{:S(2)}) async-start(), calls=%async_computation.21 | async-start | bytes 1310720 | tf_op jit(solution)/shard_map/all_gather | solution.py:154
  436.1 8.6 copy-start.3
  456.2 13.2 copy-start.54
  456.2 127.0 %all-to-all-start.1 = ((bf16[32,96,1024]{2,1,0:T(8,128)(2,1)}), bf16[32,96,1024]{2,1,0:T(8,128)(2,1)}, u32[]{:S(2)}, u32[]{:S(2)}) async-start(bf16[32,96,1024]{2,1,0:T(8,128)(2,1)} %convolution_convert_fusion), calls=%async_computation.1 | async-start | bytes 12582912 | tf_op jit(solution)/shard_map/all_to_all | solution.py:163
  583.2 14.6 copy-start.25
  624.5 79.7 %copy-start.57 = (bf16[1,512,1024]{2,1,0:T(8,128)(2,1)S(1)}, bf16[1,512,1024]{2,1,0:T(8,128)(2,1)}, u32[]{:S(2)}) copy-start(bf16[1,512,1024]{2,1,0:T(8,128)(2,1)} %all-gather.26.cloned.1.call-done) | copy-start | bytes 3145732
  624.5 83.7 %slice-start = ((s8[6291456]{0:T(1024)(128)(4,1)}), s8[4194304]{0:T(1024)(128)(4,1)S(1)}, s32[]{:S(2)}) async-start(s8[6291456]{0:T(1024)(128)(4,1)} %bitcast.228), calls=%async_computation.32 | async-start | bytes 8388608
  624.5 83.7 %slice-start.2 = ((s8[6291456]{0:T(1024)(128)(4,1)}), s8[4194304]{0:T(1024)(128)(4,1)S(1)}, s32[]{:S(2)}) async-start(s8[6291456]{0:T(1024)(128)(4,1)} %bitcast.230), calls=%async_computation.34 | async-start | bytes 8388608
  732.3 82.8 %all-to-all-start.3 = ((bf16[32,96,1024]{2,1,0:T(8,128)(2,1)}), bf16[32,96,1024]{2,1,0:T(8,128)(2,1)}, u32[]{:S(2)}, u32[]{:S(2)}) async-start(bf16[32,96,1024]{2,1,0:T(8,128)(2,1)} %add_convert_fusion), calls=%async_computation.3 | async-start | bytes 12582912 | tf_op jit(solution)/shard_map/all_to_all | solution.py:215
  737.2 163.7 %reduce-scatter.12.cloned.1.call-start = ((), (), s32[]{:S(2)}) async-start(), calls=%async_computation.23 | async-start | bytes 2621440 | tf_op jit(solution)/shard_map/reduce_scatter | solution.py:266
  737.7 97.6 %copy-start.34 = (bf16[256,32]{0,1:T(8,128)(2,1)}, bf16[256,32]{0,1:T(8,128)(2,1)S(1)}, u32[]{:S(2)}) copy-start(bf16[256,32]{0,1:T(8,128)(2,1)S(1)} %multiply_convert_fusion.1) | copy-start | bytes 49156
  829.7 6.3 copy-start.17
  829.7 7.5 copy-start.8
  838.1 10.0 copy-start.14
  848.1 57.4 %reduce-scatter.10.cloned.1.call-start = ((), (), s32[]{:S(2)}) async-start(), calls=%async_computation.22 | async-start | bytes 2621440 | tf_op jit(solution)/shard_map/reduce_scatter | solution.py:263
  859.2 7.8 copy-start.21
  859.2 7.8 copy-start.23
  871.1 183.4 %all-reduce.10.cloned.1.call-start = ((), (), s32[]{:S(2)}) async-start(), calls=%async_computation.31 | async-start | bytes 1048576
  872.3 257.9 %reduce-scatter.26.cloned.1.call-start = ((), (), s32[]{:S(2)}) async-start(), calls=%async_computation.30 | async-start | bytes 2621440 | tf_op jit(solution)/shard_map/reduce_scatter | solution.py:213
  880.9 249.2 %reduce-scatter.24.cloned.1.call-start = ((), (), s32[]{:S(2)}) async-start(), calls=%async_computation.29 | async-start | bytes 2621440 | tf_op jit(solution)/shard_map/reduce_scatter | solution.py:212
  891.9 9.0 copy-start.2
  891.9 9.0 copy-start.39
  891.9 9.0 copy-start.45
  891.9 260.3 %reduce-scatter.22.cloned.1.call-start = ((), (), s32[]{:S(2)}) async-start(), calls=%async_computation.28 | async-start | bytes 2621440 | tf_op jit(solution)/shard_map/reduce_scatter | solution.py:211
  900.7 5.9 copy-start.27
  900.7 6.0 copy-start.29
  900.7 6.0 copy-start.12
  900.7 6.0 copy-start.37
  900.7 6.1 copy-start.50
  900.7 6.7 copy-start.47
  900.8 895.2 %reduce-scatter.18.cloned.1.call-start = ((), (), s32[]{:S(2)}) async-start(), calls=%async_computation.26 | async-start | bytes 2113536 | tf_op jit(solution)/shard_map/reduce_scatter | solution.py:293
  903.9 5.7 copy-start.16
  904.0 1529.9 %reduce-scatter.16.cloned.1.call-start = ((), (), s32[]{:S(2)}) async-start(), calls=%async_computation.25 | async-start | bytes 2113536 | tf_op jit(solution)/shard_map/reduce_scatter | solution.py:292
  909.6 2164.2 %reduce-scatter.20.cloned.1.call-start = ((), (), s32[]{:S(2)}) async-start(), calls=%async_computation.27 | async-start | bytes 4227072 | tf_op jit(solution)/shard_map/reduce_scatter | solution.py:294
  912.5 6.1 copy-start.42
  912.5 2801.6 %reduce-scatter.14.cloned.1.call-start = ((), (), s32[]{:S(2)}) async-start(), calls=%async_computation.24 | async-start | bytes 4227072 | tf_op jit(solution)/shard_map/reduce_scatter | solution.py:291
  921.7 140.2 %copy-start.55 = (f32[64]{0:T(128)S(1)}, f32[64]{0:T(128)}, u32[]{:S(2)}) copy-start(f32[64]{0:T(128)} %get-tuple-element.20) | copy-start | bytes 772
  921.7 207.3 %copy-start.49 = (f32[256]{0:T(256)S(1)}, f32[256]{0:T(256)}, u32[]{:S(2)}) copy-start(f32[256]{0:T(256)} %copy-done.48) | copy-start | bytes 3076
  (20 other events, 66.1 us)
Sparse Core Ops, SparseCore 0:
  10.8 66.0 all-gather.9
  79.7 61.0 all-gather.13
  143.0 21.6 all-gather.11
  167.5 65.3 all-gather.17
  235.0 23.5 all-gather.15
  261.4 65.9 all-gather.19
  351.6 24.0 all-gather.21
  377.4 24.5 all-gather.23
  403.7 24.5 all-gather.25
  848.2 25.2 reduce-scatter.11
  876.1 29.4 reduce-scatter.9
  910.2 144.2 all-reduce.9
  1057.5 29.8 reduce-scatter.25
  1090.3 29.5 reduce-scatter.23
  1122.8 29.4 reduce-scatter.21
  1155.0 640.9 reduce-scatter.17
  1798.9 634.9 reduce-scatter.15
  2436.7 637.1 reduce-scatter.19
  3076.9 637.0 reduce-scatter.13
where the time goes:
time: 3730 us; the launch traced here: 3720 us
  waiting for transfers between devices  3130 us (84%)
  blocking collectives  260 us (7%)
  matrix products  159 us (4%)
  local copies, waits for them, and re-layouts  91.7 us (2%)
  other arithmetic  47.7 us (1%)
    reduce_scatter x1, waiting for transfers between devices, per_device(): lax.psum_scatter(grad_v_w, ('expert', 'fsdp'), scatter_dimension=0, tiled...  644 us
    reduce_scatter x1, waiting for transfers between devices, per_device(): lax.psum_scatter(grad_q_w, ('expert', 'fsdp'), scatter_dimension=0, tiled...  640 us
    reduce_scatter x1, waiting for transfers between devices, per_device(): lax.psum_scatter(grad_o_w, ('expert', 'fsdp'), scatter_dimension=0, tiled...  640 us
    reduce_scatter x1, waiting for transfers between devices, per_device(): lax.psum_scatter(grad_k_w, ('expert', 'fsdp'), scatter_dimension=0, tiled...  638 us
    unnamed x20, waiting for transfers between devices  137 us
    all_gather x1, blocking collectives, per_device(): lax.all_gather(w_router, ('expert', 'fsdp'), axis=0, tiled=True)  113 us
    all_to_all x1, blocking collectives, per_device(): lax.all_to_all(sent_grads, 'expert', split_axis=0, concat_axis=0, tiled=T...  79.7 us
  transfers between devices with their start and end apart: 22, of which 15 were waited for; matrix products, arithmetic and copies ran while one was open for 4% of the time, Pallas kernels for 0%

commit v1 on v0

v1 whole, which is shorter than its diff:
```python
import math

import jax
import jax.numpy as jnp
from jax import lax
from jax.sharding import Mesh, PartitionSpec as P

HEAD = 64
EXPERTS = 32
MOST = 96
EPS = 1e-06
NEG = -1e30
NY, NX, NC, NZ = 4, 4, 2, 4
ALL = ("y", "x", "c", "z")
BF = jnp.bfloat16
F32 = jnp.float32


def mm(a, b):
    return jnp.dot(a, b, preferred_element_type=F32)


def shift(values, axis, step):
    size = lax.axis_size(axis)
    return lax.ppermute(values, axis, [(i, (i + step) % size) for i in range(size)])


def normed(values):
    scale = lax.rsqrt(jnp.mean(values * values, axis=-1, keepdims=True) + EPS)
    return values * scale, scale


def norm_back(grad, unit, scale, gain):
    by_gain = grad * gain
    return scale * (by_gain - unit * jnp.mean(by_gain * unit, axis=-1, keepdims=True))


def rotate(values, cosine, sine):
    half = values.shape[-1] // 2
    first = values[..., :half]
    second = values[..., half:]
    return jnp.concatenate(
        [first * cosine - second * sine, second * cosine + first * sine], axis=-1
    )


def rotation(position):
    steps = jnp.arange(HEAD // 2, dtype=F32)
    freq = jnp.exp(steps * (-2.0 * math.log(10000.0) / HEAD))
    angle = position.astype(F32)[:, None] * freq[None, :]
    return jnp.cos(angle)[:, None, :], jnp.sin(angle)[:, None, :]


def in_order(blocks, place):
    return jnp.take(jnp.stack(blocks), (place - jnp.arange(len(blocks))) % len(blocks), axis=0)


def attention_forward(tokens, position, w_qkv, g_attn, g_query, g_key):
    length = tokens.shape[0]
    unit, _ = normed(tokens.astype(F32))
    first = (unit * g_attn).astype(BF)
    raw = mm(first, w_qkv)
    q_raw = raw[:, :256].reshape(length, 4, HEAD)
    k_raw = raw[:, 256:384].reshape(length, 2, HEAD)
    values = raw[:, 384:].astype(BF).reshape(length, 2, HEAD)
    cosine, sine = rotation(position)
    q_unit, q_scale = normed(q_raw)
    k_unit, k_scale = normed(k_raw)
    queries = rotate(q_unit * g_query, cosine, sine).astype(BF).reshape(length, 2, 2, HEAD)
    keys = rotate(k_unit * g_key, cosine, sine).astype(BF)
    index = jnp.arange(length, dtype=jnp.int32)
    distance = index[:, None] - index[None, :]
    allowed = (distance >= 0) & (distance <= position[:, None])
    scores = jnp.einsum("qkgd,skd->kgqs", queries, keys, preferred_element_type=F32) * HEAD**-0.5
    scores = jnp.where(allowed, scores, NEG)
    largest = jnp.max(scores, axis=-1, keepdims=True)
    log_total = largest + jnp.log(jnp.sum(jnp.exp(scores - largest), axis=-1, keepdims=True))
    probs = jnp.exp(scores - log_total)
    mixed = jnp.einsum("kgqs,skd->qkgd", probs.astype(BF), values, preferred_element_type=F32)
    kept = (unit, first, q_unit, q_scale, k_unit, k_scale, queries, keys, values, probs, cosine, sine)
    return mixed.astype(BF).reshape(length, 256), kept


def attention_backward(grad_mixed, kept, w_qkv, g_query, g_key):
    unit, first, q_unit, q_scale, k_unit, k_scale, queries, keys, values, probs, cosine, sine = kept
    length = grad_mixed.shape[0]
    grad_mixed = grad_mixed.reshape(length, 2, 2, HEAD)
    grad_probs = jnp.einsum("qkgd,skd->kgqs", grad_mixed, values, preferred_element_type=F32)
    delta = jnp.sum(probs * grad_probs, axis=-1, keepdims=True)
    grad_scores = (probs * (grad_probs - delta)).astype(BF)
    scale = HEAD**-0.5
    grad_q = jnp.einsum("kgqs,skd->qkgd", grad_scores, keys, preferred_element_type=F32) * scale
    grad_k = jnp.einsum("kgqs,qkgd->skd", grad_scores, queries, preferred_element_type=F32) * scale
    grad_v = jnp.einsum("kgqs,qkgd->skd", probs.astype(BF), grad_mixed, preferred_element_type=F32)
    grad_q = rotate(grad_q.reshape(length, 4, HEAD).astype(BF).astype(F32), cosine, -sine)
    grad_k = rotate(grad_k.astype(BF).astype(F32), cosine, -sine)
    grad_g_query = jnp.sum(grad_q * q_unit, axis=(0, 1))
    grad_g_key = jnp.sum(grad_k * k_unit, axis=(0, 1))
    grad_q = norm_back(grad_q, q_unit, q_scale, g_query).astype(BF)
    grad_k = norm_back(grad_k, k_unit, k_scale, g_key).astype(BF)
    grad_raw = jnp.concatenate(
        [grad_q.reshape(length, 256), grad_k.reshape(length, 128), grad_v.astype(BF).reshape(length, 128)],
        axis=1,
    )
    grad_first = mm(grad_raw, w_qkv.T)
    grad_w = mm(first.T, grad_raw)
    grad_g_attn = jnp.sum(grad_first * unit, axis=0)
    return grad_first.astype(BF), grad_w.astype(BF), grad_g_attn, grad_g_query, grad_g_key


def pick_rows(routes, expert):
    hit = jnp.any(routes == expert, axis=1)
    rank = jnp.cumsum(hit.astype(jnp.int32)) - 1
    slots = jnp.arange(MOST, dtype=jnp.int32)[:, None]
    return ((rank[None, :] == slots) & hit[None, :]).astype(BF)


def one_expert(second, dout, picks, expert, w_gu, w_down, w_router):
    rows = jnp.concatenate([mm(p, s).astype(BF) for p, s in zip(picks, second)])
    grads = jnp.concatenate([mm(p, g) for p, g in zip(picks, dout)])
    router = jax.nn.softmax(mm(rows, w_router), axis=-1)
    mine = (jnp.arange(EXPERTS, dtype=jnp.int32) == expert).astype(F32)
    gate = jnp.sum(router * mine, axis=-1, keepdims=True)
    both = mm(rows, w_gu)
    gate_pre, up_pre = both[:, :512], both[:, 512:]
    sig = jax.nn.sigmoid(gate_pre)
    silu = gate_pre * sig
    hidden = (silu * up_pre).astype(BF)
    out = mm(hidden, w_down).astype(BF).astype(F32)
    grad_gate = jnp.sum(out * grads, axis=-1, keepdims=True)
    result = (out * gate).astype(BF)
    dy = (grads * gate).astype(BF)
    grad_hidden = mm(dy, w_down.T).astype(BF).astype(F32)
    grad_gp = (grad_hidden * up_pre * sig * (1.0 + gate_pre * (1.0 - sig))).astype(BF)
    grad_up = (grad_hidden * silu).astype(BF)
    grad_both = jnp.concatenate([grad_gp, grad_up], axis=1)
    grad_logits = (router * (mine - gate) * grad_gate).astype(BF)
    back = (mm(grad_both, w_gu.T) + mm(grad_logits, w_router.T)).astype(BF)
    grad_w_gu = mm(rows.T, grad_both).astype(BF)
    grad_w_down = mm(hidden.T, dy).astype(BF)
    grad_w_router = mm(rows.T, grad_logits)
    return result, back, grad_w_gu, grad_w_down, grad_w_router


def spread_rows(values):
    own_x = [values] + [shift(values, "y", k) for k in range(1, NY)]
    return own_x + [shift(v, "c", 1) for v in own_x]


def collect_rows(blocks):
    over = [shift(b, "c", 1) for b in blocks[NY:]]
    mine = [(a.astype(F32) + b.astype(F32)).astype(BF) for a, b in zip(blocks[:NY], over)]
    back = [mine[0]] + [shift(mine[k], "y", -k) for k in range(1, NY)]
    total = back[0].astype(F32)
    for b in back[1:]:
        total = total + b.astype(F32)
    return total


def add_up(blocks):
    total = blocks[0].astype(F32)
    for b in blocks[1:]:
        total = total + b.astype(F32)
    return total


def block_of(values, place, size):
    return lax.dynamic_slice_in_dim(values, (place % NZ) * size, size, axis=0)


def per_device(
    tokens,
    segments,
    positions,
    routes,
    w_query,
    w_key,
    w_value,
    w_output,
    w_router,
    w_gate,
    w_up,
    w_down,
    g_attn,
    g_ffn,
    g_query,
    g_key,
    cotangent,
):
    y, x, c, z = (lax.axis_index(a) for a in ALL)
    devices = NY * NX * NC * NZ

    token_parts = [tokens] + [shift(tokens, "z", k) for k in range(1, NZ)]
    position_parts = [positions] + [shift(positions, "z", k) for k in range(1, NZ)]
    by_head = jnp.concatenate(
        [w_query.reshape(8, NZ, 256), w_key.reshape(8, NZ, 128), w_value.reshape(8, NZ, 128)], axis=2
    ).transpose(1, 0, 2)
    w_qkv = lax.all_to_all(
        jnp.broadcast_to(by_head[None], (devices // NZ, NZ, 8, 512)).reshape(devices, 8, 512), ALL, 0, 0
    ).reshape(1024, 512)
    out_router = lax.all_gather(jnp.concatenate([w_output, w_router], axis=1), ALL, axis=0, tiled=True)
    w_out, w_rout = out_router[:, :1024], out_router[:, 1024:]
    dout = spread_rows(cotangent)
    routes_all = spread_rows(routes)
    gu_own = jnp.concatenate([w_gate[0], w_up[0]], axis=1)
    gu_z = jnp.stack([gu_own] + [shift(gu_own, "z", k) for k in range(1, NZ)])
    gu = [gu_z] + [shift(gu_z, "x", j) for j in range(1, NX)]
    down_own = w_down[0]
    down_x = jnp.stack([down_own] + [shift(down_own, "x", j) for j in range(1, NX)])
    down = [down_x] + [shift(down_x, "z", k) for k in range(1, NZ)]

    sequence = in_order(token_parts, z).reshape(1024, 1024)
    position = in_order(position_parts, z).reshape(1024)
    mixed_heads, kept = attention_forward(sequence, position, w_qkv, g_attn, g_query, g_key)
    mixed = (
        lax.all_to_all(mixed_heads.reshape(NZ, 256, 256), "z", 0, 0).transpose(1, 0, 2).reshape(256, 1024)
    )
    middle = tokens.astype(F32) + mm(mixed, w_out)
    unit, scale = normed(middle)
    second = spread_rows((unit * g_ffn).astype(BF))

    results, backs, picks = [], [], []
    grads_gu, grads_down = [], []
    grad_router = 0.0
    for j in range(NX):
        expert = (y * NX + (x - j) % NX) * NC + c
        w_gu = in_order([gu[j][k] for k in range(NZ)], z).reshape(1024, 1024)
        w_dn = in_order([down[k][j] for k in range(NZ)], z).reshape(512, 1024)
        pick = [pick_rows(r, expert) for r in routes_all]
        result, back, grad_gu, grad_dn, grad_r = one_expert(second, dout, pick, expert, w_gu, w_dn, w_rout)
        results.append(result.reshape(8, MOST, 1024))
        backs.append(back.reshape(8, MOST, 1024))
        picks.append(pick)
        grads_gu.append(grad_gu)
        grads_down.append(grad_dn)
        grad_router = grad_router + grad_r
    picks = [jnp.concatenate([picks[j][b] for j in range(NX)]) for b in range(8)]

    def to_tokens(rows):
        return [mm(picks[b].T, jnp.concatenate([r[b] for r in rows])).astype(BF) for b in range(8)]

    grad_second = collect_rows(to_tokens(backs))
    mixture = collect_rows(to_tokens(results))
    output = (middle + mixture).astype(BF)

    grad_out = cotangent.astype(F32)
    grad_middle = grad_out + norm_back(grad_second, unit, scale, g_ffn)
    grad_g_ffn = jnp.sum(grad_second * unit, axis=0)
    da = grad_middle.astype(BF)
    grad_out_w = jnp.concatenate([mm(mixed.T, da), grad_router], axis=1).astype(BF)
    grad_out_parts = lax.all_to_all(grad_out_w.reshape(devices, 8, 1056), ALL, 0, 0)
    dense = jnp.sum(grad_out_parts.astype(F32), axis=0)
    grad_mixed = mm(da, w_out.T).astype(BF)
    grad_heads = lax.all_to_all(grad_mixed.reshape(256, NZ, 256).transpose(1, 0, 2), "z", 0, 0).reshape(
        1024, 256
    )
    grad_first, grad_w, grad_g_attn, grad_g_query, grad_g_key = attention_backward(
        grad_heads, kept, w_qkv, g_query, g_key
    )
    grad_first = jnp.sum(
        lax.all_to_all(grad_first.reshape(NZ, 256, 1024), "z", 0, 0).astype(F32), axis=0
    )
    unit_first, scale_first = normed(tokens.astype(F32))
    grad_tokens = (grad_middle + norm_back(grad_first, unit_first, scale_first, g_attn)).astype(BF)

    grad_w = lax.all_to_all(grad_w.reshape(devices, 8, 512), ALL, 0, 0)
    grad_w = jnp.sum(grad_w.astype(F32).reshape(devices // NZ, NZ, 8, 512), axis=0)
    grad_query = grad_w[:, :, :256].transpose(1, 0, 2).reshape(8, 1024)
    grad_key = grad_w[:, :, 256:384].transpose(1, 0, 2).reshape(8, 512)
    grad_value = grad_w[:, :, 384:].transpose(1, 0, 2).reshape(8, 512)
    gains = jnp.concatenate([grad_g_attn, grad_g_ffn, grad_g_query, grad_g_key]).reshape(1, 17, 128)
    gains = lax.all_to_all(jnp.broadcast_to(gains, (devices, 17, 128)), ALL, 0, 0)
    gains = jnp.sum(gains, axis=0).reshape(17 * 128)

    grad_gu = add_up([grads_gu[0]] + [shift(grads_gu[j], "x", -j) for j in range(1, NX)]).astype(BF)
    grad_gu = add_up(
        [block_of(grad_gu, z, 256)] + [shift(block_of(grad_gu, z + k, 256), "z", k) for k in range(1, NZ)]
    )
    stacked = jnp.concatenate(grads_down, axis=1)
    grad_dn = add_up(
        [block_of(stacked, z, 128)] + [shift(block_of(stacked, z + k, 128), "z", k) for k in range(1, NZ)]
    ).astype(BF)
    grad_dn = add_up(
        [grad_dn[:, :1024]]
        + [shift(grad_dn[:, 1024 * j : 1024 * (j + 1)], "x", -j) for j in range(1, NX)]
    )
    return (
        output,
        grad_tokens,
        grad_query,
        grad_key,
        grad_value,
        dense[:, :1024],
        dense[:, 1024:],
        grad_gu[None, :, :512],
        grad_gu[None, :, 512:],
        grad_dn[None],
        gains[:1024],
        gains[1024:2048],
        gains[2048:2112],
        gains[2112:2176],
    )


def solution(mesh):
    grid = Mesh(mesh.devices.reshape(NY, NX, NC, NZ), ALL)
    rows = P(ALL, None)
    line = P(ALL)
    expert = P(("y", "x", "c"), "z", None)
    in_specs = (rows, line, line, rows) + (rows,) * 5 + (expert,) * 3 + (P(),) * 4 + (rows,)
    out_specs = (rows,) * 7 + (expert,) * 3 + (P(),) * 4
    return jax.shard_map(
        per_device, mesh=grid, in_specs=in_specs, out_specs=out_specs, check_vma=False
    )
```

time: 3730 us -> 855 us (0.23)
  waiting for transfers between devices: 3130 us -> 236 us
  blocking collectives: 260 us -> 0 us
  starting transfers between devices: 16.7 us -> 160 us
  other arithmetic: 47.7 us -> 141 us
  matrix products: 159 us -> 197 us
    reduce_scatter x9 -> x0, waiting for transfers between devices: 2590 us -> none  [the longest x1 644 us: per_device(): lax.psum_scatter(grad_v_w, ('expert', 'fsdp'), scatter_dimension=0, tiled...]
    all_gather x9 -> x1, waiting for transfers between devices: 283 us -> 0.01 us  [per_device(): lax.all_gather(jnp.concatenate([w_output, w_router], axis=1), ALL, axis=0...]
    ppermute x0 -> x65, waiting for transfers between devices: none -> 214 us  [shift(): lax.ppermute(values, axis, [(i, (i + step) % size) for i in range(size)])]
    unnamed x20 -> x1, waiting for transfers between devices: 137 us -> 0.02 us
    all_gather x1 -> x0, blocking collectives: 113 us -> none  [per_device(): lax.all_gather(w_router, ('expert', 'fsdp'), axis=0, tiled=True)]
    all_to_all x3 -> x7, waiting for transfers between devices: 124 us -> 21.9 us  [the longest x1 8.11 us: per_device(): lax.all_to_all(grad_first.reshape(NZ, 256, 1024), 'z', 0, 0).astype(F32)]
    all_to_all x1 -> x0, blocking collectives: 79.7 us -> none  [per_device(): lax.all_to_all(sent_grads, 'expert', split_axis=0, concat_axis=0, tiled=T...]
    ppermute x0 -> x65, starting transfers between devices: none -> 73.2 us  [shift(): lax.ppermute(values, axis, [(i, (i + step) % size) for i in range(size)])]
  transfers between devices with their start and end apart: 22 -> 73, of which waited for: 15 -> 20; matrix products, arithmetic and copies ran while one was open for 4% -> 42% of each run, Pallas kernels for 0% -> 0%
where the time goes in v1:
time: 855 us; the launch traced here: 842 us
  waiting for transfers between devices  236 us (28%)
  matrix products  197 us (23%)
  starting transfers between devices  160 us (19%)
  other arithmetic  141 us (16%)
  local copies, waits for them, and re-layouts  90.2 us (11%)
  between operations  18.3 us (2%)
    ppermute x65, waiting for transfers between devices, shift(): lax.ppermute(values, axis, [(i, (i + step) % size) for i in range(size)])  214 us
    dot_general x122, matrix products, mm(): return jnp.dot(a, b, preferred_element_type=F32)  161 us
    ppermute x65, starting transfers between devices, shift(): lax.ppermute(values, axis, [(i, (i + step) % size) for i in range(size)])  73.2 us
    all_to_all x1, starting transfers between devices, per_device(): lax.all_to_all(jnp.broadcast_to(gains, (devices, 17, 128)), ALL, 0, 0)  45.6 us
    another operation x66, other arithmetic  32.9 us
    and x32, other arithmetic, pick_rows(): return ((rank[None, :] == slots) & hit[None, :]).astype(BF)  29.4 us
    gather x10, local copies, waits for them, and re-layouts, in_order(): jnp.take(jnp.stack(blocks), (place - jnp.arange(len(blocks))) % len(block...  28.5 us
    another operation x48, local copies, waits for them, and re-layouts  17.6 us
  transfers between devices with their start and end apart: 73, of which 20 were waited for; matrix products, arithmetic and copies ran while one was open for 42% of the time, Pallas kernels for 0%

profile of v1, /device:TPU:0, one launch (start us, length us, event | category | flops | bytes accessed | tf_op | source)
XLA Modules:
  0.0 842.3 jit_solution(7208915965593434575)
XLA Ops:
  14.9 2.9 collective-permute-start.8
  21.0 7.5 all-to-all-start
  49.4 2.7 collective-permute-start.25
  154.1 3.2 collective-permute-start.41
  157.3 7.5 collective-permute-done.1
  166.8 2.7 pad_maximum_fusion.2
  171.8 6.1 collective-permute-done.39
  192.7 6.0 collective-permute-done.22
  199.3 2.6 pad_maximum_fusion.3
  202.5 3.6 gather_fusion.2
  233.2 3.1 fusion.112
  238.0 3.1 fusion.4
  241.1 3.7 exponential_reduce_fusion
  247.2 4.8 fusion.58
  255.3 5.9 all-to-all-start.1
  265.4 2.8 collective-permute-start.31
  293.9 2.9 gather_fusion.3
  296.7 3.0 pad_maximum_fusion.11
  299.7 2.8 gather_fusion.7
  302.5 2.8 gather_fusion.9
  305.3 2.8 gather_fusion.5
  308.1 4.3 broadcast_select_fusion.8
  312.4 46.3 %collective-permute-done.31 = bf16[4,256,1024]{2,1,0:T(8,128)(2,1)} collective-permute-done((bf16[4,256,1024]{2,1,0:T(8,128)(2,1)S(1)}, bf16[4,256,1024]{2,1,0:T(8,128)(2,1)}, u32[]{:S(2)}, u32[]{:S(2)}) %collective-permute-start.31) | collective-permute-done | bytes 2097184 | tf_op jit(solution)/shard_map/ppermute | solution.py:25
  358.8 3.6 gather_fusion.8
  362.4 3.6 gather_fusion.6
  366.7 3.6 gather_fusion.4
  370.3 7.1 broadcast_select_fusion.3
  377.5 2.6 multiply_reduce_fusion.5
  383.6 11.7 %collective-permute-done.11 = bf16[256,1024]{1,0:T(8,128)(2,1)S(1)} collective-permute-done((bf16[256,1024]{1,0:T(8,128)(2,1)S(1)}, bf16[256,1024]{1,0:T(8,128)(2,1)S(1)}, u32[]{:S(2)}, u32[]{:S(2)}) %collective-permute-start.11) | collective-permute-done | bytes 524320 | tf_op jit(solution)/shard_map/ppermute | solution.py:25
  396.9 10.6 %collective-permute-done.7 = bf16[256,1024]{1,0:T(8,128)(2,1)S(1)} collective-permute-done((bf16[256,1024]{1,0:T(8,128)(2,1)S(1)}, bf16[256,1024]{1,0:T(8,128)(2,1)S(1)}, u32[]{:S(2)}, u32[]{:S(2)}) %collective-permute-start.7) | collective-permute-done | bytes 524320 | tf_op jit(solution)/shard_map/ppermute | solution.py:25
  434.5 3.5 fusion.30
  438.0 3.6 fusion.13
  441.6 3.0 convolution_convert_fusion.9
  449.2 3.6 fusion.34
  452.8 3.5 fusion.15
  456.4 3.4 convolution_convert_fusion.8
  463.7 3.2 convolution_convert_fusion.3
  488.8 2.9 collective-permute-start.50
  497.1 17.7 %collective-permute-done.52 = bf16[256,1024]{1,0:T(8,128)(2,1)S(1)} collective-permute-done((bf16[256,1024]{1,0:T(8,128)(2,1)S(1)}, bf16[256,1024]{1,0:T(8,128)(2,1)S(1)}, u32[]{:S(2)}, u32[]{:S(2)}) %collective-permute-start.52) | collective-permute-done | bytes 524320 | tf_op jit(solution)/shard_map/ppermute | solution.py:25
  516.8 2.6 collective-permute-start.34
  520.9 16.3 %collective-permute-done.38 = bf16[256,1024]{1,0:T(8,128)(2,1)S(1)} collective-permute-done((bf16[256,1024]{1,0:T(8,128)(2,1)S(1)}, bf16[256,1024]{1,0:T(8,128)(2,1)S(1)}, u32[]{:S(2)}, u32[]{:S(2)}) %collective-permute-start.38) | collective-permute-done | bytes 524320 | tf_op jit(solution)/shard_map/ppermute | solution.py:25
  537.2 3.5 collective-permute-start.60
  540.7 3.1 multiply_add_fusion
  545.4 3.5 all-to-all-start.2
  548.9 4.5 convolution_convert_fusion.2
  553.4 6.0 all-to-all-done.2
  560.8 11.1 %fusion.63 = bf16[2,64,1024]{2,1,0:T(8,128)(2,1)} fusion(bf16[1024,2,2,64]{0,3,2,1:T(8,128)(2,1)} %reshape_reshape.7, f32[2,1024,1024,2]{2,1,3,0:T(8,128)} %copy-done, f32[2,2,1024]{2,1,0:T(2,128)} %copy-done.67, pred[1024,1024]{0,1:T(8,128)(4,1)S(1)} %fusion.7), kind=kOutput, calls=%fused_computation.206 | convolution fusion | flops 553779200 | bytes 18628608 | tf_op jit(solution)/shard_map/kgqs,qkgd->skd/dot_general | solution.py:94
  571.9 13.6 %fusion = (f32[2,2,1024]{2,1,0:T(2,128)}, f32[2,1024,1024,2]{2,1,3,0:T(8,128)}) fusion(f32[2,1024,1024,2]{2,1,3,0:T(8,128)} %copy-done, f32[2,2,1024]{2,1,0:T(2,128)} %copy-done.67, pred[1024,1024]{0,1:T(8,128)(4,1)S(1)} %fusion.7, bf16[1024,2,64,1]{0,2,3,1:T(8,128)(2,1)} %bitcast.501, bf16[1024,2,2,64]{0,3,2,1:T(8,128)(2,1)} %reshape_reshape.7), kind=kOutput, calls=%fused_computation.12 | convolution fusion | flops 557838336 | bytes 35422208 | tf_op jit(solution)/shard_map/qkgd,skd->kgqs/dot_general | solution.py:88
  585.5 8.5 %fusion.2 = bf16[2,2,1024,1024]{2,3,1,0:T(8,128)(2,1)S(1)} fusion(f32[2,1024,1024,2]{2,1,3,0:T(8,128)} %get-tuple-element.213, f32[2,1024,1024,2]{2,1,3,0:T(8,128)S(1)} %bitcast.465, f32[2,2,1024]{2,1,0:T(2,128)} %get-tuple-element.212, f32[2,2,1024]{2,1,0:T(2,128)} %copy-done.67, pred[1024,1024]{0,1:T(8,128)(4,1)S(1)} %fusion.7), kind=kLoop, calls=%fused_computation.14 | loop fusion | flops 25165824 | bytes 43024384 | tf_op jit(solution)/shard_map/convert_element_type | solution.py:90
  594.1 2.7 fusion.62
  602.3 4.6 multiply_reduce_fusion
  609.3 12.1 %all-to-all-start.4 = ((bf16[128,8,512]{2,1,0:T(8,128)(2,1)}), bf16[128,8,512]{2,1,0:T(8,128)(2,1)}, u32[]{:S(2)}, u32[]{:S(2)}) async-start(bf16[128,8,512]{2,1,0:T(8,128)(2,1)} %fusion.40), calls=%async_computation.4 | async-start | bytes 2097152 | tf_op jit(solution)/shard_map/all_to_all | solution.py:266
  626.2 4.6 convolution_convert_fusion.1
  631.9 7.8 all-to-all-done.4
  641.0 45.6 %all-to-all-start.6 = ((f32[128,17,128]{2,1,0:T(8,128)}), f32[128,17,128]{2,1,0:T(8,128)}, u32[]{:S(2)}, u32[]{:S(2)}) async-start(f32[128,17,128]{2,1,0:T(8,128)} %broadcast_in_dim.57), calls=%async_computation.6 | async-start | bytes 3145728 | tf_op jit(solution)/shard_map/all_to_all | solution.py:272
  686.7 2.8 add_convert_fusion.5
  694.4 51.6 %collective-permute-done.62 = bf16[128,1024]{1,0:T(8,128)(2,1)} collective-permute-done((bf16[128,1024]{1,0:T(8,128)(2,1)S(1)}, bf16[128,1024]{1,0:T(8,128)(2,1)}, u32[]{:S(2)}, u32[]{:S(2)}) %collective-permute-start.62) | collective-permute-done | bytes 262176 | tf_op jit(solution)/shard_map/ppermute | solution.py:25
  745.9 2.7 collective-permute-start.63
  748.6 4.7 all-to-all-start.3
  753.6 2.7 copy.96
  758.5 5.2 add_convert_fusion
  773.1 8.1 all-to-all-done.3
  781.3 7.1 all-to-all-start.5
  792.6 34.5 %collective-permute-done.57 = bf16[256,1024]{1,0:T(8,128)(2,1)} collective-permute-done((bf16[256,1024]{1,0:T(8,128)(2,1)}, bf16[256,1024]{1,0:T(8,128)(2,1)}, u32[]{:S(2)}, u32[]{:S(2)}) %collective-permute-start.57) | collective-permute-done | bytes 524320 | tf_op jit(solution)/shard_map/ppermute | solution.py:25
  (1156 shorter events, 334.4 us)
Async XLA Ops:
  7.2 370.3 %all-gather.2.cloned.1.call-start = ((), (), s32[]{:S(2)}) async-start(), calls=%async_computation.7 | async-start | bytes 2377728 | tf_op jit(solution)/shard_map/all_gather | solution.py:201
  7.2 39.9 %collective-permute-start.3 = (s32[256]{0:T(256)}, s32[256]{0:T(256)S(1)}, u32[]{:S(2)}, u32[]{:S(2)}) collective-permute-start(s32[256]{0:T(256)} %param.22), channel_id=1, source_target_pairs={{0,1},{1,2},{2,3},{3,0},{4,5},{5,6},{6,7},{7,4},{8,9},{9,10},{10,1... | collective-permute-start | bytes 3080 | tf_op jit(solution)/shard_map/ppermute | solution.py:25
  9.3 37.8 %collective-permute-start.5 = (s32[256]{0:T(256)}, s32[256]{0:T(256)S(1)}, u32[]{:S(2)}, u32[]{:S(2)}) collective-permute-start(s32[256]{0:T(256)} %param.22), channel_id=1, source_target_pairs={{0,3},{1,0},{2,1},{3,2},{4,7},{5,4},{6,5},{7,6},{8,11},{9,8},{10,9... | collective-permute-start | bytes 3080 | tf_op jit(solution)/shard_map/ppermute | solution.py:25
  11.5 37.9 %collective-permute-start.4 = (s32[256]{0:T(256)}, s32[256]{0:T(256)S(1)}, u32[]{:S(2)}, u32[]{:S(2)}) collective-permute-start(s32[256]{0:T(256)} %param.22), channel_id=1, source_target_pairs={{0,2},{1,3},{2,0},{3,1},{4,6},{5,7},{6,4},{7,5},{8,10},{9,11},{10,... | collective-permute-start | bytes 3080 | tf_op jit(solution)/shard_map/ppermute | solution.py:25
  13.3 41.4 %collective-permute-start.6 = (s32[256,8]{0,1:T(8,128)}, s32[256,8]{0,1:T(8,128)S(1)}, u32[]{:S(2)}, u32[]{:S(2)}) collective-permute-start(s32[256,8]{0,1:T(8,128)} %param.23), channel_id=1, source_target_pairs={{0,32},{32,64},{64,96},{96,0},{1,33},{33,65},{65,97},{97,1},{2,34}... | collective-permute-start | bytes 24584 | tf_op jit(solution)/shard_map/ppermute | solution.py:25
  14.9 43.0 %collective-permute-start.8 = (s32[256,8]{0,1:T(8,128)}, s32[256,8]{0,1:T(8,128)S(1)}, u32[]{:S(2)}, u32[]{:S(2)}) collective-permute-start(s32[256,8]{0,1:T(8,128)} %param.23), channel_id=1, source_target_pairs={{0,64},{32,96},{64,0},{96,32},{1,65},{33,97},{65,1},{97,33},{2,66}... | collective-permute-start | bytes 24584 | tf_op jit(solution)/shard_map/ppermute | solution.py:25
  21.0 212.2 %all-to-all-start = ((bf16[128,8,512]{2,1,0:T(8,128)(2,1)}), bf16[128,8,512]{2,1,0:T(8,128)(2,1)}, u32[]{:S(2)}, u32[]{:S(2)}) async-start(bf16[128,8,512]{2,1,0:T(8,128)(2,1)} %bitcast.9), calls=%async_computation | async-start | bytes 2097152 | tf_op jit(solution)/shard_map/all_to_all | solution.py:198
  47.1 14.1 %collective-permute-start.12 = (s32[256,8]{0,1:T(8,128)S(1)}, s32[256,8]{0,1:T(8,128)S(1)}, u32[]{:S(2)}, u32[]{:S(2)}) collective-permute-start(s32[256,8]{0,1:T(8,128)S(1)} %copy-done.269), channel_id=1, source_target_pairs={{0,4},{4,0},{1,5},{5,1},{2,6},{6,2},{3,7},{7,3},{8,12},{12,8},{9,1... | collective-permute-start | bytes 24584 | tf_op jit(solution)/shard_map/ppermute | solution.py:25
  47.1 20.7 %collective-permute-start.10 = (s32[256,8]{0,1:T(8,128)S(1)}, s32[256,8]{0,1:T(8,128)}, u32[]{:S(2)}, u32[]{:S(2)}) collective-permute-start(s32[256,8]{0,1:T(8,128)S(1)} %copy-done.269), channel_id=1, source_target_pairs={{0,96},{32,0},{64,32},{96,64},{1,97},{33,1},{65,33},{97,65},{2,98}... | collective-permute-start | bytes 24584 | tf_op jit(solution)/shard_map/ppermute | solution.py:25
  49.4 100.1 %collective-permute-start.25 = (bf16[128,1024]{1,0:T(8,128)(2,1)S(1)}, bf16[128,1024]{1,0:T(8,128)(2,1)S(1)}, u32[]{:S(2)}, u32[]{:S(2)}) collective-permute-start(bf16[128,1024]{1,0:T(8,128)(2,1)S(1)} %bitcast.491), channel_id=1, source_target_pairs={{0,24},{8,0},{16,8},{24,16},{1,25},{9,1},{17,9},{25,17},{2,26},{10... | collective-permute-start | bytes 786440 | tf_op jit(solution)/shard_map/ppermute | solution.py:25
  54.7 96.9 %collective-permute-start.24 = (bf16[128,1024]{1,0:T(8,128)(2,1)S(1)}, bf16[128,1024]{1,0:T(8,128)(2,1)S(1)}, u32[]{:S(2)}, u32[]{:S(2)}) collective-permute-start(bf16[128,1024]{1,0:T(8,128)(2,1)S(1)} %bitcast.492), channel_id=1, source_target_pairs={{0,16},{8,24},{16,0},{24,8},{1,17},{9,25},{17,1},{25,9},{2,18},{10... | collective-permute-start | bytes 786440 | tf_op jit(solution)/shard_map/ppermute | solution.py:25
  57.9 95.0 %collective-permute-start.23 = (bf16[128,1024]{1,0:T(8,128)(2,1)S(1)}, bf16[128,1024]{1,0:T(8,128)(2,1)S(1)}, u32[]{:S(2)}, u32[]{:S(2)}) collective-permute-start(bf16[128,1024]{1,0:T(8,128)(2,1)S(1)} %bitcast.493), channel_id=1, source_target_pairs={{0,8},{8,16},{16,24},{24,0},{1,9},{9,17},{17,25},{25,1},{2,10},{10... | collective-permute-start | bytes 786440 | tf_op jit(solution)/shard_map/ppermute | solution.py:25
  61.2 92.8 %collective-permute-start = (bf16[256,1024]{1,0:T(8,128)(2,1)S(1)}, bf16[256,1024]{1,0:T(8,128)(2,1)S(1)}, u32[]{:S(2)}, u32[]{:S(2)}) collective-permute-start(bf16[256,1024]{1,0:T(8,128)(2,1)S(1)} %copy-done.8), channel_id=1, source_target_pairs={{0,1},{1,2},{2,3},{3,0},{4,5},{5,6},{6,7},{7,4},{8,9},{9,10},{10,1... | collective-permute-start | bytes 1572872 | tf_op jit(solution)/shard_map/ppermute | solution.py:25
  96.5 19.7 %collective-permute-start.18 = (s32[256,8]{0,1:T(8,128)}, s32[256,8]{0,1:T(8,128)}, u32[]{:S(2)}, u32[]{:S(2)}) collective-permute-start(s32[256,8]{0,1:T(8,128)} %collective-permute-done.10), channel_id=1, source_target_pairs={{0,4},{4,0},{1,5},{5,1},{2,6},{6,2},{3,7},{7,3},{8,12},{12,8},{9,1... | collective-permute-start | bytes 24584 | tf_op jit(solution)/shard_map/ppermute | solution.py:25
  116.2 41.1 %collective-permute-start.2 = (bf16[256,1024]{1,0:T(8,128)(2,1)S(1)}, bf16[256,1024]{1,0:T(8,128)(2,1)}, u32[]{:S(2)}, u32[]{:S(2)}) collective-permute-start(bf16[256,1024]{1,0:T(8,128)(2,1)S(1)} %copy-done.8), channel_id=1, source_target_pairs={{0,3},{1,0},{2,1},{3,2},{4,7},{5,4},{6,5},{7,6},{8,11},{9,8},{10,9... | collective-permute-start | bytes 1572872 | tf_op jit(solution)/shard_map/ppermute | solution.py:25
  149.5 15.2 %collective-permute-start.1 = (bf16[256,1024]{1,0:T(8,128)(2,1)S(1)}, bf16[256,1024]{1,0:T(8,128)(2,1)S(1)}, u32[]{:S(2)}, u32[]{:S(2)}) collective-permute-start(bf16[256,1024]{1,0:T(8,128)(2,1)S(1)} %copy-done.8), channel_id=1, source_target_pairs={{0,2},{1,3},{2,0},{3,1},{4,6},{5,7},{6,4},{7,5},{8,10},{9,11},{10,... | collective-permute-start | bytes 1572872 | tf_op jit(solution)/shard_map/ppermute | solution.py:25
  151.6 26.3 %collective-permute-start.39 = (bf16[256,1024]{1,0:T(8,128)(2,1)}, bf16[256,1024]{1,0:T(8,128)(2,1)}, u32[]{:S(2)}, u32[]{:S(2)}) collective-permute-start(bf16[256,1024]{1,0:T(8,128)(2,1)} %param.36), channel_id=1, source_target_pairs={{0,32},{32,64},{64,96},{96,0},{1,33},{33,65},{65,97},{97,1},{2,34}... | collective-permute-start | bytes 1572872 | tf_op jit(solution)/shard_map/ppermute | solution.py:25
  152.9 57.3 %collective-permute-start.42 = (bf16[256,1024]{1,0:T(8,128)(2,1)}, bf16[256,1024]{1,0:T(8,128)(2,1)}, u32[]{:S(2)}, u32[]{:S(2)}) collective-permute-start(bf16[256,1024]{1,0:T(8,128)(2,1)} %param.36), channel_id=1, source_target_pairs={{0,4},{4,0},{1,5},{5,1},{2,6},{6,2},{3,7},{7,3},{8,12},{12,8},{9,1... | collective-permute-start | bytes 1572872 | tf_op jit(solution)/shard_map/ppermute | solution.py:25
  154.1 52.0 %collective-permute-start.41 = (bf16[256,1024]{1,0:T(8,128)(2,1)}, bf16[256,1024]{1,0:T(8,128)(2,1)}, u32[]{:S(2)}, u32[]{:S(2)}) collective-permute-start(bf16[256,1024]{1,0:T(8,128)(2,1)} %param.36), channel_id=1, source_target_pairs={{0,96},{32,0},{64,32},{96,64},{1,97},{33,1},{65,33},{97,65},{2,98}... | collective-permute-start | bytes 1572872 | tf_op jit(solution)/shard_map/ppermute | solution.py:25
  157.3 26.2 %collective-permute-start.40 = (bf16[256,1024]{1,0:T(8,128)(2,1)}, bf16[256,1024]{1,0:T(8,128)(2,1)}, u32[]{:S(2)}, u32[]{:S(2)}) collective-permute-start(bf16[256,1024]{1,0:T(8,128)(2,1)} %param.36), channel_id=1, source_target_pairs={{0,64},{32,96},{64,0},{96,32},{1,65},{33,97},{65,1},{97,33},{2,66}... | collective-permute-start | bytes 1572872 | tf_op jit(solution)/shard_map/ppermute | solution.py:25
  164.7 25.3 %collective-permute-start.21 = (bf16[256,1024]{1,0:T(8,128)(2,1)}, bf16[256,1024]{1,0:T(8,128)(2,1)}, u32[]{:S(2)}, u32[]{:S(2)}) collective-permute-start(bf16[256,1024]{1,0:T(8,128)(2,1)} %get-tuple-element.179), channel_id=1, source_target_pairs={{0,2},{1,3},{2,0},{3,1},{4,6},{5,7},{6,4},{7,5},{8,10},{9,11},{10,... | collective-permute-start | bytes 1572872 | tf_op jit(solution)/shard_map/ppermute | solution.py:25
  177.9 12.6 %collective-permute-start.20 = (bf16[256,1024]{1,0:T(8,128)(2,1)}, bf16[256,1024]{1,0:T(8,128)(2,1)S(1)}, u32[]{:S(2)}, u32[]{:S(2)}) collective-permute-start(bf16[256,1024]{1,0:T(8,128)(2,1)} %get-tuple-element.179), channel_id=1, source_target_pairs={{0,1},{1,2},{2,3},{3,0},{4,5},{5,6},{6,7},{7,4},{8,9},{9,10},{10,1... | collective-permute-start | bytes 1572872 | tf_op jit(solution)/shard_map/ppermute | solution.py:25
  183.5 15.2 %collective-permute-start.22 = (bf16[256,1024]{1,0:T(8,128)(2,1)}, bf16[256,1024]{1,0:T(8,128)(2,1)S(1)}, u32[]{:S(2)}, u32[]{:S(2)}) collective-permute-start(bf16[256,1024]{1,0:T(8,128)(2,1)} %get-tuple-element.179), channel_id=1, source_target_pairs={{0,3},{1,0},{2,1},{3,2},{4,7},{5,4},{6,5},{7,6},{8,11},{9,8},{10,9... | collective-permute-start | bytes 1572872 | tf_op jit(solution)/shard_map/ppermute | solution.py:25
  190.0 91.0 %collective-permute-start.28 = (bf16[4,128,1024]{2,1,0:T(8,128)(2,1)}, bf16[4,128,1024]{2,1,0:T(8,128)(2,1)}, u32[]{:S(2)}, u32[]{:S(2)}) collective-permute-start(bf16[4,128,1024]{2,1,0:T(8,128)(2,1)} %fusion.105), channel_id=1, source_target_pairs={{0,3},{1,0},{2,1},{3,2},{4,7},{5,4},{6,5},{7,6},{8,11},{9,8},{10,9... | collective-permute-start | bytes 3145736 | tf_op jit(solution)/shard_map/ppermute | solution.py:25
  190.5 97.6 %collective-permute-start.27 = (bf16[4,128,1024]{2,1,0:T(8,128)(2,1)}, bf16[4,128,1024]{2,1,0:T(8,128)(2,1)}, u32[]{:S(2)}, u32[]{:S(2)}) collective-permute-start(bf16[4,128,1024]{2,1,0:T(8,128)(2,1)} %fusion.105), channel_id=1, source_target_pairs={{0,2},{1,3},{2,0},{3,1},{4,6},{5,7},{6,4},{7,5},{8,10},{9,11},{10,... | collective-permute-start | bytes 3145736 | tf_op jit(solution)/shard_map/ppermute | solution.py:25
  198.7 91.6 %collective-permute-start.26 = (bf16[4,128,1024]{2,1,0:T(8,128)(2,1)}, bf16[4,128,1024]{2,1,0:T(8,128)(2,1)}, u32[]{:S(2)}, u32[]{:S(2)}) collective-permute-start(bf16[4,128,1024]{2,1,0:T(8,128)(2,1)} %fusion.105), channel_id=1, source_target_pairs={{0,1},{1,2},{2,3},{3,0},{4,5},{5,6},{6,7},{7,4},{8,9},{9,10},{10,1... | collective-permute-start | bytes 3145736 | tf_op jit(solution)/shard_map/ppermute | solution.py:25
  206.1 59.4 %collective-permute-start.44 = (bf16[256,1024]{1,0:T(8,128)(2,1)}, bf16[256,1024]{1,0:T(8,128)(2,1)}, u32[]{:S(2)}, u32[]{:S(2)}) collective-permute-start(bf16[256,1024]{1,0:T(8,128)(2,1)} %collective-permute-done.40), channel_id=1, source_target_pairs={{0,4},{4,0},{1,5},{5,1},{2,6},{6,2},{3,7},{7,3},{8,12},{12,8},{9,1... | collective-permute-start | bytes 1572872 | tf_op jit(solution)/shard_map/ppermute | solution.py:25
  210.2 51.0 %collective-permute-start.43 = (bf16[256,1024]{1,0:T(8,128)(2,1)}, bf16[256,1024]{1,0:T(8,128)(2,1)}, u32[]{:S(2)}, u32[]{:S(2)}) collective-permute-start(bf16[256,1024]{1,0:T(8,128)(2,1)} %collective-permute-done.39), channel_id=1, source_target_pairs={{0,4},{4,0},{1,5},{5,1},{2,6},{6,2},{3,7},{7,3},{8,12},{12,8},{9,1... | collective-permute-start | bytes 1572872 | tf_op jit(solution)/shard_map/ppermute | solution.py:25
  255.3 122.1 %all-to-all-start.1 = ((bf16[4,256,256]{1,2,0:T(8,128)(2,1)}), bf16[4,256,256]{1,2,0:T(8,128)(2,1)}, u32[]{:S(2)}, u32[]{:S(2)}) async-start(bf16[4,256,256]{1,2,0:T(8,128)(2,1)} %copy.83), calls=%async_computation.1 | async-start | bytes 1048576 | tf_op jit(solution)/shard_map/all_to_all | solution.py:216
  261.2 11.1 %collective-permute-start.45 = (bf16[256,1024]{1,0:T(8,128)(2,1)}, bf16[256,1024]{1,0:T(8,128)(2,1)S(1)}, u32[]{:S(2)}, u32[]{:S(2)}) collective-permute-start(bf16[256,1024]{1,0:T(8,128)(2,1)} %collective-permute-done.41), channel_id=1, source_target_pairs={{0,4},{4,0},{1,5},{5,1},{2,6},{6,2},{3,7},{7,3},{8,12},{12,8},{9,1... | collective-permute-start | bytes 1572872 | tf_op jit(solution)/shard_map/ppermute | solution.py:25
  265.4 93.3 %collective-permute-start.31 = (bf16[4,256,1024]{2,1,0:T(8,128)(2,1)S(1)}, bf16[4,256,1024]{2,1,0:T(8,128)(2,1)}, u32[]{:S(2)}, u32[]{:S(2)}) collective-permute-start(bf16[4,256,1024]{2,1,0:T(8,128)(2,1)S(1)} %copy-done.13), channel_id=1, source_target_pairs={{0,24},{8,0},{16,8},{24,16},{1,25},{9,1},{17,9},{25,17},{2,26},{10... | collective-permute-start | bytes 6291464 | tf_op jit(solution)/shard_map/ppermute | solution.py:25
  272.3 90.1 %collective-permute-start.30 = (bf16[4,256,1024]{2,1,0:T(8,128)(2,1)S(1)}, bf16[4,256,1024]{2,1,0:T(8,128)(2,1)}, u32[]{:S(2)}, u32[]{:S(2)}) collective-permute-start(bf16[4,256,1024]{2,1,0:T(8,128)(2,1)S(1)} %copy-done.13), channel_id=1, source_target_pairs={{0,16},{8,24},{16,0},{24,8},{1,17},{9,25},{17,1},{25,9},{2,18},{10... | collective-permute-start | bytes 6291464 | tf_op jit(solution)/shard_map/ppermute | solution.py:25
  281.0 85.7 %collective-permute-start.29 = (bf16[4,256,1024]{2,1,0:T(8,128)(2,1)S(1)}, bf16[4,256,1024]{2,1,0:T(8,128)(2,1)}, u32[]{:S(2)}, u32[]{:S(2)}) collective-permute-start(bf16[4,256,1024]{2,1,0:T(8,128)(2,1)S(1)} %copy-done.13), channel_id=1, source_target_pairs={{0,8},{8,16},{16,24},{24,0},{1,9},{9,17},{17,25},{25,1},{2,10},{10... | collective-permute-start | bytes 6291464 | tf_op jit(solution)/shard_map/ppermute | solution.py:25
  380.4 28.9 %collective-permute-start.13 = (bf16[256,1024]{1,0:T(8,128)(2,1)S(1)}, bf16[256,1024]{1,0:T(8,128)(2,1)S(1)}, u32[]{:S(2)}, u32[]{:S(2)}) collective-permute-start(bf16[256,1024]{1,0:T(8,128)(2,1)S(1)} %multiply_convert_fusion.10), channel_id=1, source_target_pairs={{0,4},{4,0},{1,5},{5,1},{2,6},{6,2},{3,7},{7,3},{8,12},{12,8},{9,1... | collective-permute-start | bytes 1572872 | tf_op jit(solution)/shard_map/ppermute | solution.py:25
  380.5 14.8 %collective-permute-start.11 = (bf16[256,1024]{1,0:T(8,128)(2,1)S(1)}, bf16[256,1024]{1,0:T(8,128)(2,1)S(1)}, u32[]{:S(2)}, u32[]{:S(2)}) collective-permute-start(bf16[256,1024]{1,0:T(8,128)(2,1)S(1)} %multiply_convert_fusion.10), channel_id=1, source_target_pairs={{0,96},{32,0},{64,32},{96,64},{1,97},{33,1},{65,33},{97,65},{2,98}... | collective-permute-start | bytes 1572872 | tf_op jit(solution)/shard_map/ppermute | solution.py:25
  380.6 16.4 %collective-permute-start.9 = (bf16[256,1024]{1,0:T(8,128)(2,1)S(1)}, bf16[256,1024]{1,0:T(8,128)(2,1)S(1)}, u32[]{:S(2)}, u32[]{:S(2)}) collective-permute-start(bf16[256,1024]{1,0:T(8,128)(2,1)S(1)} %multiply_convert_fusion.10), channel_id=1, source_target_pairs={{0,64},{32,96},{64,0},{96,32},{1,65},{33,97},{65,1},{97,33},{2,66}... | collective-permute-start | bytes 1572872 | tf_op jit(solution)/shard_map/ppermute | solution.py:25
  380.6 26.9 %collective-permute-start.7 = (bf16[256,1024]{1,0:T(8,128)(2,1)S(1)}, bf16[256,1024]{1,0:T(8,128)(2,1)S(1)}, u32[]{:S(2)}, u32[]{:S(2)}) collective-permute-start(bf16[256,1024]{1,0:T(8,128)(2,1)S(1)} %multiply_convert_fusion.10), channel_id=1, source_target_pairs={{0,32},{32,64},{64,96},{96,0},{1,33},{33,65},{65,97},{97,1},{2,34}... | collective-permute-start | bytes 1572872 | tf_op jit(solution)/shard_map/ppermute | solution.py:25
  395.3 17.0 %collective-permute-start.19 = (bf16[256,1024]{1,0:T(8,128)(2,1)S(1)}, bf16[256,1024]{1,0:T(8,128)(2,1)S(1)}, u32[]{:S(2)}, u32[]{:S(2)}) collective-permute-start(bf16[256,1024]{1,0:T(8,128)(2,1)S(1)} %collective-permute-done.11), channel_id=1, source_target_pairs={{0,4},{4,0},{1,5},{5,1},{2,6},{6,2},{3,7},{7,3},{8,12},{12,8},{9,1... | collective-permute-start | bytes 1572872 | tf_op jit(solution)/shard_map/ppermute | solution.py:25
  396.9 15.2 %collective-permute-start.17 = (bf16[256,1024]{1,0:T(8,128)(2,1)S(1)}, bf16[256,1024]{1,0:T(8,128)(2,1)S(1)}, u32[]{:S(2)}, u32[]{:S(2)}) collective-permute-start(bf16[256,1024]{1,0:T(8,128)(2,1)S(1)} %collective-permute-done.9), channel_id=1, source_target_pairs={{0,4},{4,0},{1,5},{5,1},{2,6},{6,2},{3,7},{7,3},{8,12},{12,8},{9,1... | collective-permute-start | bytes 1572872 | tf_op jit(solution)/shard_map/ppermute | solution.py:25
  473.9 11.7 %collective-permute-start.37 = (bf16[256,1024]{1,0:T(8,128)(2,1)S(1)}, bf16[256,1024]{1,0:T(8,128)(2,1)S(1)}, u32[]{:S(2)}, u32[]{:S(2)}) collective-permute-start(bf16[256,1024]{1,0:T(8,128)(2,1)S(1)} %convolution_convert_fusion.25), channel_id=1, source_target_pairs={{0,4},{4,0},{1,5},{5,1},{2,6},{6,2},{3,7},{7,3},{8,12},{12,8},{9,1... | collective-permute-start | bytes 1572872 | tf_op jit(solution)/shard_map/ppermute | solution.py:25
  474.9 13.9 %collective-permute-start.35 = (bf16[256,1024]{1,0:T(8,128)(2,1)S(1)}, bf16[256,1024]{1,0:T(8,128)(2,1)S(1)}, u32[]{:S(2)}, u32[]{:S(2)}) collective-permute-start(bf16[256,1024]{1,0:T(8,128)(2,1)S(1)} %convolution_convert_fusion.27), channel_id=1, source_target_pairs={{0,4},{4,0},{1,5},{5,1},{2,6},{6,2},{3,7},{7,3},{8,12},{12,8},{9,1... | collective-permute-start | bytes 1572872 | tf_op jit(solution)/shard_map/ppermute | solution.py:25
  475.5 16.2 %collective-permute-start.33 = (bf16[256,1024]{1,0:T(8,128)(2,1)S(1)}, bf16[256,1024]{1,0:T(8,128)(2,1)S(1)}, u32[]{:S(2)}, u32[]{:S(2)}) collective-permute-start(bf16[256,1024]{1,0:T(8,128)(2,1)S(1)} %convolution_convert_fusion.29), channel_id=1, source_target_pairs={{0,4},{4,0},{1,5},{5,1},{2,6},{6,2},{3,7},{7,3},{8,12},{12,8},{9,1... | collective-permute-start | bytes 1572872 | tf_op jit(solution)/shard_map/ppermute | solution.py:25
  488.0 26.8 %collective-permute-start.52 = (bf16[256,1024]{1,0:T(8,128)(2,1)S(1)}, bf16[256,1024]{1,0:T(8,128)(2,1)S(1)}, u32[]{:S(2)}, u32[]{:S(2)}) collective-permute-start(bf16[256,1024]{1,0:T(8,128)(2,1)S(1)} %add_convert_fusion.6), channel_id=1, source_target_pairs={{0,32},{32,64},{64,96},{96,0},{1,33},{33,65},{65,97},{97,1},{2,34}... | collective-permute-start | bytes 1572872 | tf_op jit(solution)/shard_map/ppermute | solution.py:25
  488.8 26.3 %collective-permute-start.50 = (bf16[256,1024]{1,0:T(8,128)(2,1)S(1)}, bf16[256,1024]{1,0:T(8,128)(2,1)S(1)}, u32[]{:S(2)}, u32[]{:S(2)}) collective-permute-start(bf16[256,1024]{1,0:T(8,128)(2,1)S(1)} %add_convert_fusion.7), channel_id=1, source_target_pairs={{0,64},{32,96},{64,0},{96,32},{1,65},{33,97},{65,1},{97,33},{2,66}... | collective-permute-start | bytes 1572872 | tf_op jit(solution)/shard_map/ppermute | solution.py:25
  491.7 25.1 %collective-permute-start.48 = (bf16[256,1024]{1,0:T(8,128)(2,1)S(1)}, bf16[256,1024]{1,0:T(8,128)(2,1)S(1)}, u32[]{:S(2)}, u32[]{:S(2)}) collective-permute-start(bf16[256,1024]{1,0:T(8,128)(2,1)S(1)} %add_convert_fusion.8), channel_id=1, source_target_pairs={{0,96},{32,0},{64,32},{96,64},{1,97},{33,1},{65,33},{97,65},{2,98}... | collective-permute-start | bytes 1572872 | tf_op jit(solution)/shard_map/ppermute | solution.py:25
  493.1 138.0 %collective-permute-start.59 = (bf16[128,4096]{1,0:T(8,128)(2,1)}, bf16[128,4096]{1,0:T(8,128)(2,1)}, u32[]{:S(2)}, u32[]{:S(2)}) collective-permute-start(bf16[128,4096]{1,0:T(8,128)(2,1)} %get-tuple-element.52), channel_id=1, source_target_pairs={{0,1},{1,2},{2,3},{3,0},{4,5},{5,6},{6,7},{7,4},{8,9},{9,10},{10,1... | collective-permute-start | bytes 3145736 | tf_op jit(solution)/shard_map/ppermute | solution.py:25
  495.7 191.0 %collective-permute-start.61 = (bf16[128,4096]{1,0:T(8,128)(2,1)}, bf16[128,4096]{1,0:T(8,128)(2,1)}, u32[]{:S(2)}, u32[]{:S(2)}) collective-permute-start(bf16[128,4096]{1,0:T(8,128)(2,1)} %get-tuple-element.53), channel_id=1, source_target_pairs={{0,3},{1,0},{2,1},{3,2},{4,7},{5,4},{6,5},{7,6},{8,11},{9,8},{10,9... | collective-permute-start | bytes 3145736 | tf_op jit(solution)/shard_map/ppermute | solution.py:25
  514.8 22.4 %collective-permute-start.38 = (bf16[256,1024]{1,0:T(8,128)(2,1)S(1)}, bf16[256,1024]{1,0:T(8,128)(2,1)S(1)}, u32[]{:S(2)}, u32[]{:S(2)}) collective-permute-start(bf16[256,1024]{1,0:T(8,128)(2,1)S(1)} %add_convert_fusion.11), channel_id=1, source_target_pairs={{0,32},{32,64},{64,96},{96,0},{1,33},{33,65},{65,97},{97,1},{2,34}... | collective-permute-start | bytes 1572872 | tf_op jit(solution)/shard_map/ppermute | solution.py:25
  515.1 25.6 %collective-permute-start.36 = (bf16[256,1024]{1,0:T(8,128)(2,1)S(1)}, bf16[256,1024]{1,0:T(8,128)(2,1)S(1)}, u32[]{:S(2)}, u32[]{:S(2)}) collective-permute-start(bf16[256,1024]{1,0:T(8,128)(2,1)S(1)} %add_convert_fusion.12), channel_id=1, source_target_pairs={{0,64},{32,96},{64,0},{96,32},{1,65},{33,97},{65,1},{97,33},{2,66}... | collective-permute-start | bytes 1572872 | tf_op jit(solution)/shard_map/ppermute | solution.py:25
  516.8 23.9 %collective-permute-start.34 = (bf16[256,1024]{1,0:T(8,128)(2,1)S(1)}, bf16[256,1024]{1,0:T(8,128)(2,1)S(1)}, u32[]{:S(2)}, u32[]{:S(2)}) collective-permute-start(bf16[256,1024]{1,0:T(8,128)(2,1)S(1)} %add_convert_fusion.13), channel_id=1, source_target_pairs={{0,96},{32,0},{64,32},{96,64},{1,97},{33,1},{65,33},{97,65},{2,98}... | collective-permute-start | bytes 1572872 | tf_op jit(solution)/shard_map/ppermute | solution.py:25
  537.2 149.5 %collective-permute-start.60 = (bf16[128,4096]{1,0:T(8,128)(2,1)}, bf16[128,4096]{1,0:T(8,128)(2,1)}, u32[]{:S(2)}, u32[]{:S(2)}) collective-permute-start(bf16[128,4096]{1,0:T(8,128)(2,1)} %get-tuple-element.54), channel_id=1, source_target_pairs={{0,2},{1,3},{2,0},{3,1},{4,6},{5,7},{6,4},{7,5},{8,10},{9,11},{10,... | collective-permute-start | bytes 3145736 | tf_op jit(solution)/shard_map/ppermute | solution.py:25
  545.4 13.9 %all-to-all-start.2 = ((bf16[4,256,256]{2,1,0:T(8,128)(2,1)}), bf16[4,256,256]{2,1,0:T(8,128)(2,1)S(1)}, u32[]{:S(2)}, u32[]{:S(2)}) async-start(bf16[4,256,256]{2,1,0:T(8,128)(2,1)} %bitcast.485), calls=%async_computation.2 | async-start | bytes 1048576 | tf_op jit(solution)/shard_map/all_to_all | solution.py:254
  609.3 30.4 %all-to-all-start.4 = ((bf16[128,8,512]{2,1,0:T(8,128)(2,1)}), bf16[128,8,512]{2,1,0:T(8,128)(2,1)}, u32[]{:S(2)}, u32[]{:S(2)}) async-start(bf16[128,8,512]{2,1,0:T(8,128)(2,1)} %fusion.40), calls=%async_computation.4 | async-start | bytes 2097152 | tf_op jit(solution)/shard_map/all_to_all | solution.py:266
  622.0 136.5 %collective-permute-start.53 = (bf16[1024,1024]{1,0:T(8,128)(2,1)}, bf16[1024,1024]{1,0:T(8,128)(2,1)}, u32[]{:S(2)}, u32[]{:S(2)}) collective-permute-start(bf16[1024,1024]{1,0:T(8,128)(2,1)} %convolution_convert_fusion.3), channel_id=1, source_target_pairs={{0,24},{8,0},{16,8},{24,16},{1,25},{9,1},{17,9},{25,17},{2,26},{10... | collective-permute-start | bytes 6291464 | tf_op jit(solution)/shard_map/ppermute | solution.py:25
  624.2 134.3 %collective-permute-start.54 = (bf16[1024,1024]{1,0:T(8,128)(2,1)}, bf16[1024,1024]{1,0:T(8,128)(2,1)}, u32[]{:S(2)}, u32[]{:S(2)}) collective-permute-start(bf16[1024,1024]{1,0:T(8,128)(2,1)} %convolution_convert_fusion.2), channel_id=1, source_target_pairs={{0,16},{8,24},{16,0},{24,8},{1,17},{9,25},{17,1},{25,9},{2,18},{10... | collective-permute-start | bytes 6291464 | tf_op jit(solution)/shard_map/ppermute | solution.py:25
  631.1 127.4 %collective-permute-start.55 = (bf16[1024,1024]{1,0:T(8,128)(2,1)}, bf16[1024,1024]{1,0:T(8,128)(2,1)}, u32[]{:S(2)}, u32[]{:S(2)}) collective-permute-start(bf16[1024,1024]{1,0:T(8,128)(2,1)} %convolution_convert_fusion.1), channel_id=1, source_target_pairs={{0,8},{8,16},{16,24},{24,0},{1,9},{9,17},{17,25},{25,1},{2,10},{10... | collective-permute-start | bytes 6291464 | tf_op jit(solution)/shard_map/ppermute | solution.py:25
  641.0 107.6 %all-to-all-start.6 = ((f32[128,17,128]{2,1,0:T(8,128)}), f32[128,17,128]{2,1,0:T(8,128)}, u32[]{:S(2)}, u32[]{:S(2)}) async-start(f32[128,17,128]{2,1,0:T(8,128)} %broadcast_in_dim.57), calls=%async_computation.6 | async-start | bytes 3145728 | tf_op jit(solution)/shard_map/all_to_all | solution.py:272
  690.4 55.5 %collective-permute-start.62 = (bf16[128,1024]{1,0:T(8,128)(2,1)S(1)}, bf16[128,1024]{1,0:T(8,128)(2,1)}, u32[]{:S(2)}, u32[]{:S(2)}) collective-permute-start(bf16[128,1024]{1,0:T(8,128)(2,1)S(1)} %get-tuple-element.151), channel_id=1, source_target_pairs={{0,24},{8,0},{16,8},{24,16},{1,25},{9,1},{17,9},{25,17},{2,26},{10... | collective-permute-start | bytes 786440 | tf_op jit(solution)/shard_map/ppermute | solution.py:25
  694.3 62.0 %collective-permute-start.64 = (bf16[128,1024]{1,0:T(8,128)(2,1)}, bf16[128,1024]{1,0:T(8,128)(2,1)}, u32[]{:S(2)}, u32[]{:S(2)}) collective-permute-start(bf16[128,1024]{1,0:T(8,128)(2,1)} %get-tuple-element.152), channel_id=1, source_target_pairs={{0,8},{8,16},{16,24},{24,0},{1,9},{9,17},{17,25},{25,1},{2,10},{10... | collective-permute-start | bytes 786440 | tf_op jit(solution)/shard_map/ppermute | solution.py:25
  748.6 32.6 %all-to-all-start.3 = ((bf16[4,256,1024]{2,1,0:T(8,128)(2,1)}), bf16[4,256,1024]{2,1,0:T(8,128)(2,1)}, u32[]{:S(2)}, u32[]{:S(2)}) async-start(bf16[4,256,1024]{2,1,0:T(8,128)(2,1)} %bitcast.132), calls=%async_computation.3 | async-start | bytes 4194304 | tf_op jit(solution)/shard_map/all_to_all | solution.py:261
  766.2 26.3 %collective-permute-start.56 = (bf16[256,1024]{1,0:T(8,128)(2,1)}, bf16[256,1024]{1,0:T(8,128)(2,1)}, u32[]{:S(2)}, u32[]{:S(2)}) collective-permute-start(bf16[256,1024]{1,0:T(8,128)(2,1)} %get-tuple-element.72), channel_id=1, source_target_pairs={{0,1},{1,2},{2,3},{3,0},{4,5},{5,6},{6,7},{7,4},{8,9},{9,10},{10,1... | collective-permute-start | bytes 1572872 | tf_op jit(solution)/shard_map/ppermute | solution.py:25
  768.2 24.3 %collective-permute-start.58 = (bf16[256,1024]{1,0:T(8,128)(2,1)}, bf16[256,1024]{1,0:T(8,128)(2,1)}, u32[]{:S(2)}, u32[]{:S(2)}) collective-permute-start(bf16[256,1024]{1,0:T(8,128)(2,1)} %get-tuple-element.73), channel_id=1, source_target_pairs={{0,3},{1,0},{2,1},{3,2},{4,7},{5,4},{6,5},{7,6},{8,11},{9,8},{10,9... | collective-permute-start | bytes 1572872 | tf_op jit(solution)/shard_map/ppermute | solution.py:25
  769.4 57.7 %collective-permute-start.57 = (bf16[256,1024]{1,0:T(8,128)(2,1)}, bf16[256,1024]{1,0:T(8,128)(2,1)}, u32[]{:S(2)}, u32[]{:S(2)}) collective-permute-start(bf16[256,1024]{1,0:T(8,128)(2,1)} %get-tuple-element.74), channel_id=1, source_target_pairs={{0,2},{1,3},{2,0},{3,1},{4,6},{5,7},{6,4},{7,5},{8,10},{9,11},{10,... | collective-permute-start | bytes 1572872 | tf_op jit(solution)/shard_map/ppermute | solution.py:25
  781.3 52.4 %all-to-all-start.5 = ((bf16[128,8,1056]{2,1,0:T(8,128)(2,1)}), bf16[128,8,1056]{2,1,0:T(8,128)(2,1)S(1)}, u32[]{:S(2)}, u32[]{:S(2)}) async-start(bf16[128,8,1056]{2,1,0:T(8,128)(2,1)} %copy.96), calls=%async_computation.5 | async-start | bytes 4718592 | tf_op jit(solution)/shard_map/all_to_all | solution.py:251
  (310 other events, 6749.4 us)
Sparse Core Ops, SparseCore 0:
  19.2 72.7 all-gather.1
